TPU v7x, 512 devices: a whole 4x8x8 slice. The times are simulated.
512 devices in a mesh: bal: 32 (over x, y), uly: 8 (over z), cfg: 2 (over core).
Axes of the slice: x: 4, y: 8, z: 8, core: 2. Of those that a mesh axis runs over, the one named last changes fastest.
Arguments:
- hidden: bfloat16 [2, 16384, 3072], P('cfg', ('bal', 'uly')), may hold values from -32 to 32
- w_qkv: bfloat16 [3072, 6144], P(None, ('uly', 'cfg')), may hold values from -0.109375 to 0.109375
- q_gain: float32 [2048], P('uly'), may hold values from 2 to 4
- cache_k: bfloat16 [2, 16384, 2048], P('cfg', 'bal', 'uly'), may hold values from -80 to 80
- cache_v: bfloat16 [2, 16384, 2048], P('cfg', 'bal', 'uly'), may hold values from -6 to 6
- fresh_list: int32 [2, 32, 8, 4], P('cfg', 'bal', 'uly'), may hold values from 0 to 8, as said below
Outputs:
- fresh_out: bfloat16 [2, 32, 8, 32, 2048], P('cfg', 'bal', 'uly')
Inputs may be any that keep to these rules, and one draw needn't show every extreme that they name: `fresh_list`: for each branch and uly index, the 32 lists along bal name 32 blocks in all, at most 4 on one device, and some device names exactly 4, some none; within a list the used entries are distinct, rising and come first, and the unused ones hold 8.
All inputs are finite; a program needn't handle non-finite values.
Results may differ from a plain program's by a relative error of at most 0.014.
Values may be sent and summed in bfloat16 or wider, within the bound.
A program may use at most 64 MiB of HBM per device.

v0:
```python
import math

import jax
import jax.numpy as jnp
from jax import lax
from jax.sharding import PartitionSpec as P

HEAD_DIM = 128
BLOCK = 8


def normalize(values):
    return values * lax.rsqrt(jnp.mean(values * values, axis=-1, keepdims=True) + 1e-06)


def finish(projected, gains):
    query = (normalize(projected[:, :, 0]) * gains).astype(jnp.bfloat16)
    return jnp.stack(
        [query, projected[:, :, 1].astype(jnp.bfloat16), projected[:, :, 2].astype(jnp.bfloat16)],
        axis=2,
    )


def layout(id_lists, tok_count, block_rows):
    bal_size, uly_size, list_len = id_lists.shape
    block_count = tok_count // block_rows
    counts = jnp.sum((id_lists < block_count).astype(jnp.int32), axis=2)
    row_ends = jnp.cumsum(counts, axis=0) * block_rows
    row_start = row_ends - counts * block_rows
    owner_ids = jnp.arange(bal_size, dtype=jnp.int32)[:, None, None]
    slot_ids = jnp.arange(block_rows, dtype=jnp.int32)[None, None, :]
    uly_ids = jnp.arange(uly_size, dtype=jnp.int32)[None, :, None]
    global_row = slot_ids * bal_size + owner_ids + 0 * uly_ids
    ends_t = jnp.transpose(row_ends)[None, :, None, :]
    source = jnp.sum((ends_t <= global_row[..., None]).astype(jnp.int32), axis=3)
    source_hit = (source[..., None] == jnp.arange(bal_size, dtype=jnp.int32)).astype(jnp.int32)
    local_row = global_row - jnp.sum(
        source_hit * jnp.transpose(row_start)[None, :, None, :], axis=3
    )
    chosen = jnp.sum(
        source_hit[..., None] * jnp.transpose(id_lists, (1, 0, 2))[None, :, None, :, :], axis=3
    )
    entry_hit = (
        (local_row // block_rows)[..., None] == jnp.arange(list_len, dtype=jnp.int32)
    ).astype(jnp.int32)
    block_ids = jnp.sum(entry_hit * chosen, axis=3)
    position = (
        (source * uly_size + uly_ids) * tok_count + block_ids * block_rows + local_row % block_rows
    )
    return (counts, row_start, source, local_row, position)


def on_device(hidden, w_qkv, q_gain, cache_k, cache_v, fresh_list):
    bal_size = lax.axis_size("bal")
    uly_size = lax.axis_size("uly")
    bal_index = lax.axis_index("bal")
    uly_index = lax.axis_index("uly")
    tok_count = hidden.shape[1]
    width = hidden.shape[2]
    list_len = fresh_list.shape[3]
    block_rows = BLOCK
    head_width = HEAD_DIM
    local_heads = q_gain.shape[0] // head_width
    key_rows = cache_k.shape[1]
    spread = list_len * block_rows
    pair_rows = spread // bal_size
    group_count = uly_size * block_rows
    my_list = fresh_list[0, 0, 0]
    id_lists = lax.all_gather(fresh_list.reshape(1, list_len), ("bal", "uly"), axis=0, tiled=True)
    id_lists = id_lists.reshape(bal_size, uly_size, list_len)
    counts, row_start, source, local_row, position = layout(id_lists, tok_count, block_rows)
    my_count = jnp.sum((my_list < tok_count // block_rows).astype(jnp.int32))
    my_start = row_start[bal_index, uly_index]
    row_ids = jnp.arange(spread, dtype=jnp.int32)
    row_valid = row_ids < my_count * block_rows
    list_hit = (
        (row_ids // block_rows)[:, None] == jnp.arange(list_len, dtype=jnp.int32)[None, :]
    ).astype(jnp.int32)
    block_ids = jnp.sum(list_hit * my_list[None, :], axis=1)
    tok_ids = jnp.where(row_valid, block_ids * block_rows + row_ids % block_rows, 0)
    fresh_rows = jnp.where(row_valid[:, None], hidden[0][tok_ids], 0)
    owner_ids = jnp.arange(bal_size, dtype=jnp.int32)
    pair_ids = jnp.arange(pair_rows, dtype=jnp.int32)
    take_rows = pair_ids[None, :] * bal_size + (owner_ids[:, None] - my_start) % bal_size
    outgoing = fresh_rows[take_rows]
    incoming = lax.all_to_all(outgoing, "bal", split_axis=0, concat_axis=0, tiled=True)
    slot_source = source[bal_index, uly_index]
    slot_row = local_row[bal_index, uly_index]
    flat_ids = slot_source * pair_rows + slot_row // bal_size
    selector = (flat_ids[:, None] == jnp.arange(spread, dtype=jnp.int32)[None, :]).astype(
        jnp.bfloat16
    )
    owned = jnp.dot(
        selector, incoming.reshape(spread, width), preferred_element_type=jnp.float32
    ).astype(jnp.bfloat16)
    group = lax.all_gather(owned, "uly", axis=0, tiled=True)
    gains = q_gain.reshape(local_heads, head_width)
    projected = jnp.dot(
        group, lax.all_gather(w_qkv, "cfg", axis=1, tiled=True), preferred_element_type=jnp.float32
    )
    fresh = finish(projected.reshape(group_count, local_heads, 3, head_width), gains)
    key_block = cache_k[0].reshape(key_rows, local_heads, head_width)
    value_block = cache_v[0].reshape(key_rows, local_heads, head_width)
    everything = lax.all_gather(fresh, "bal", axis=0, tiled=True)
    queries = everything[:, :, 0]
    spots = position.reshape(-1) - bal_index * key_rows
    spots = jnp.where((spots >= 0) & (spots < key_rows), spots, key_rows)
    key_block = key_block.at[spots].set(everything[:, :, 1], mode="drop")
    value_block = value_block.at[spots].set(everything[:, :, 2], mode="drop")
    normed = normalize(key_block.astype(jnp.float32)).astype(jnp.bfloat16)
    fresh_total = queries.shape[0]
    query_rows = min(512, fresh_total)
    scale = 1.0 / math.sqrt(head_width)

    def attend(query_block):
        scores = (
            jnp.einsum("qhd,khd->hqk", query_block, normed, preferred_element_type=jnp.float32)
            * scale
        )
        weights = jnp.exp(scores)
        totals = jnp.sum(weights, axis=2)
        sums = jnp.einsum(
            "hqk,khd->qhd",
            weights.astype(jnp.bfloat16),
            value_block,
            preferred_element_type=jnp.float32,
        )
        return (sums, jnp.transpose(totals))

    sums, totals = lax.map(
        attend, queries.reshape(fresh_total // query_rows, query_rows, local_heads, head_width)
    )
    sums = sums.reshape(fresh_total, local_heads * head_width)
    totals = totals.reshape(fresh_total, local_heads)
    my_sums, my_totals = (
        lax.psum_scatter(sums, "bal", scatter_dimension=0, tiled=True),
        lax.psum_scatter(totals, "bal", scatter_dimension=0, tiled=True),
    )
    attended = my_sums.reshape(group_count, local_heads, head_width) / my_totals[:, :, None]
    attended = attended.astype(jnp.bfloat16).reshape(group_count, local_heads * head_width)
    rows_back = lax.all_to_all(attended, "uly", split_axis=0, concat_axis=1, tiled=True)
    mine_start = row_start[:, uly_index][:, None]
    mine_count = counts[:, uly_index][:, None]
    back_row = pair_ids[None, :] * bal_size + (bal_index - mine_start) % bal_size
    back_valid = back_row < mine_count * block_rows
    back_slot = jnp.where(back_valid, (mine_start + back_row - bal_index) // bal_size, 0)
    leaving = jnp.where(back_valid[..., None], rows_back[back_slot], 0)
    returned_rows = lax.all_to_all(leaving, "bal", split_axis=0, concat_axis=0, tiled=True)
    returned_rows = returned_rows.reshape(spread, returned_rows.shape[2])
    final_ids = (my_start + row_ids) % bal_size * pair_rows + row_ids // bal_size
    result = jnp.where(row_valid[:, None], returned_rows[final_ids], 0)
    return result.reshape(1, 1, 1, spread, result.shape[1])


def solution(mesh):
    in_specs = (
        P("cfg", ("bal", "uly"), None),
        P(None, ("uly", "cfg")),
        P("uly"),
        P("cfg", "bal", "uly"),
        P("cfg", "bal", "uly"),
        P("cfg", "bal", "uly", None),
    )
    out_specs = P("cfg", "bal", "uly", None, None)
    return jax.shard_map(
        on_device, mesh=mesh, in_specs=in_specs, out_specs=out_specs, check_vma=False
    )
```

profile of v0, /device:TPU:2, one launch (start us, length us, event | category | flops | bytes accessed | tf_op | source)
XLA Modules:
  0.0 1463.3 jit_solution(18223976803015052469)
XLA Ops:
  6.5 0.7 all-gather.4.cloned.1.call-update
  7.3 606.1 %all-gather = s32[256,1,1,4]{3,2,1,0:T(1,128)S(1)} all-gather(s32[1,1,1,4]{3,2,1,0:T(1,128)S(1)} %copy-done.4), channel_id=2, replica_groups=mesh['bal'=32,'uly'=8,'cfg'=2] {'bal','uly'}, dimensions={0}, use_global_device_ids=true | all-gather | bytes 4112 | tf_op jit(solution)/shard_map/all_gather | solution.py:69
  613.4 4.6 fusion.15
  618.2 0.6 fusion.44
  619.8 0.7 gather_fusion
  620.5 0.7 dynamic_slice.23
  621.2 0.7 fusion.46
  622.0 0.7 gather_fusion.1
  623.2 0.7 reduce.11
  623.8 0.8 reshape.600
  624.6 83.8 %all-to-all-start = ((bf16[32,2,1536]{2,1,0:T(2,128)(2,1)}), bf16[32,2,1536]{2,1,0:T(2,128)(2,1)S(1)}, u32[]{:S(2)}, u32[]{:S(2)}) async-start(bf16[32,2,1536]{2,1,0:T(2,128)(2,1)} %reshape.600), calls=%async_computation | async-start | bytes 393216 | tf_op jit(solution)/shard_map/all_to_all | solution.py:86
  709.1 4.5 convert_reduce_fusion
  713.5 4.7 select_reduce_fusion
  718.7 25.0 %all_gather.13 = bf16[64,3072]{1,0:T(8,128)(2,1)S(1)} all-gather(bf16[8,3072]{1,0:T(8,128)(2,1)S(1)} %convolution_convert_fusion), channel_id=1, replica_groups=mesh['bal'=32,'uly'=8,'cfg'=2] {'uly'}, dimensions={0}, use_global_device_ids=true | all-gather | bytes 442368 | tf_op jit(solution)/shard_map/all_gather | solution.py:96
  743.7 3.3 fusion.49
  747.9 0.7 copy.155
  749.5 17.7 %multiply_reduce_fusion = s32[32,8,8,4]{2,3,1,0:T(4,128)S(1)} fusion(s32[8,32,4]{1,2,0:T(4,128)S(1)} %copy.158, s32[32,8,8,32]{3,2,1,0:T(8,128)S(1)} %fusion.9), kind=kLoop, calls=%fused_computation.18 | loop fusion | flops 516096 | bytes 299008 | tf_op jit(solution)/shard_map/reduce_sum | solution.py:40
  768.7 60.9 %all-gather.6.cloned.1.call-done = bf16[2048,2,3,128]{3,1,2,0:T(2,128)(2,1)} async-done(((bf16[64,2,3,128]{3,1,2,0:T(2,128)(2,1)}), bf16[2048,2,3,128]{3,1,2,0:T(2,128)(2,1)}) %all-gather.6.cloned.1.call-update) | async-done | bytes 3145744 | tf_op jit(solution)/shard_map/all_gather | solution.py:104
  829.7 3.6 fusion.48
  833.2 1.3 copy_bitcast_fusion.1
  834.5 8.6 copy.169
  843.1 59.4 %scatter_fusion.1 = bf16[512,2,128]{2,1,0:T(2,128)(2,1)S(1)} fusion(bf16[512,2,128]{2,1,0:T(2,128)(2,1)S(1)} %copy.168, s32[2048]{0:T(1024)S(1)} %bitcast.103, bf16[2048,2,128]{2,1,0:T(2,128)(2,1)S(1)} %copy.169), kind=kCustom, calls=%fused_computation.5 | custom fusion | bytes 3153920 | tf_op jit(solution)/shard_map/scatter | solution.py:109
  902.6 2.8 copy.163
  905.5 59.4 %scatter_fusion = bf16[512,2,128]{2,1,0:T(2,128)(2,1)S(1)} fusion(bf16[512,2,128]{2,1,0:T(2,128)(2,1)S(1)} %copy.162, s32[2048]{0:T(1024)S(1)} %bitcast.104, bf16[2048,2,128]{2,1,0:T(2,128)(2,1)S(1)} %copy.163), kind=kCustom, calls=%fused_computation.4 | custom fusion | bytes 3153920 | tf_op jit(solution)/shard_map/scatter | solution.py:108
  964.9 0.6 fusion.10
  965.6 0.7 fusion.11
  966.5 9.0 while.12
  967.0 0.5 convolution_bitcast_fusion.2
  967.5 1.2 copy_dynamic-update-slice_fusion.2
  969.8 1.2 copy_dynamic-update-slice_fusion.2
  972.0 1.2 copy_dynamic-update-slice_fusion.2
  974.2 1.2 copy_dynamic-update-slice_fusion.2
  975.5 1.4 copy.178
  976.9 3.1 copy.207
  980.4 213.1 %reduce-scatter.7.cloned.1.call-done = f32[64,2]{1,0:T(8,128)} async-done(((f32[2048,2]{1,0:T(8,128)}), f32[64,2]{1,0:T(8,128)}) %reduce-scatter.7.cloned.1.call-update) | async-done | bytes 528 | tf_op jit(solution)/shard_map/reduce_scatter | solution.py:137
  1193.5 224.3 %reduce-scatter.5.cloned.1.call-done = f32[64,256]{1,0:T(8,128)} async-done(((f32[2048,256]{1,0:T(8,128)}), f32[64,256]{1,0:T(8,128)}) %reduce-scatter.5.cloned.1.call-update) | async-done | bytes 65552 | tf_op jit(solution)/shard_map/reduce_scatter | solution.py:136
  1417.8 0.9 div.85
  1418.7 1.5 fusion.18
  1420.2 7.3 all-to-all-start.1
  1427.5 8.0 all-to-all-done.1
  1435.5 0.6 gather_fusion.2
  1436.3 0.6 reduce.12
  1436.9 0.7 reshape.602
  1437.6 8.2 all-to-all-start.2
  1445.8 0.8 fusion.33
  1446.6 8.3 all-to-all-done.2
  1455.1 0.7 gather_fusion.3
  1455.8 0.7 bitcast_select_fusion
  (82 shorter events, 9.8 us)
Async XLA Ops:
  6.5 613.3 %copy-start = (bf16[1,64,3072]{2,1,0:T(8,128)(2,1)S(1)}, bf16[1,64,3072]{2,1,0:T(8,128)(2,1)}, u32[]{:S(2)}) copy-start(bf16[1,64,3072]{2,1,0:T(8,128)(2,1)} %param.8) | copy-start | bytes 1179652
  6.5 0.7 copy-start.4
  6.5 737.2 %all-gather.4.cloned.1.call-start = ((), (), s32[]{:S(2)}) async-start(), calls=%async_computation.5 | async-start | bytes 7077888 | tf_op jit(solution)/shard_map/all_gather | solution.py:99
  624.6 93.7 %all-to-all-start = ((bf16[32,2,1536]{2,1,0:T(2,128)(2,1)}), bf16[32,2,1536]{2,1,0:T(2,128)(2,1)S(1)}, u32[]{:S(2)}, u32[]{:S(2)}) async-start(bf16[32,2,1536]{2,1,0:T(2,128)(2,1)} %reshape.600), calls=%async_computation | async-start | bytes 393216 | tf_op jit(solution)/shard_map/all_to_all | solution.py:86
  708.4 121.2 %all-gather.6.cloned.1.call-start = ((), (), s32[]{:S(2)}) async-start(), calls=%async_computation.6 | async-start | bytes 3244032 | tf_op jit(solution)/shard_map/all_gather | solution.py:104
  743.7 3.7 copy-start.3
  748.6 444.9 %reduce-scatter.7.cloned.1.call-start = ((), (), s32[]{:S(2)}) async-start(), calls=%async_computation.8 | async-start | bytes 1081344 | tf_op jit(solution)/shard_map/reduce_scatter | solution.py:137
  749.0 19.1 %copy-start.1 = (bf16[1,512,256]{2,1,0:T(8,128)(2,1)S(1)}, bf16[1,512,256]{2,1,0:T(8,128)(2,1)}, u32[]{:S(2)}) copy-start(bf16[1,512,256]{2,1,0:T(8,128)(2,1)} %param.12) | copy-start | bytes 786436
  749.5 18.9 %copy-start.2 = (bf16[1,512,256]{2,1,0:T(8,128)(2,1)S(1)}, bf16[1,512,256]{2,1,0:T(8,128)(2,1)}, u32[]{:S(2)}) copy-start(bf16[1,512,256]{2,1,0:T(8,128)(2,1)} %param.11) | copy-start | bytes 786436
  976.9 440.9 %reduce-scatter.5.cloned.1.call-start = ((), (), s32[]{:S(2)}) async-start(), calls=%async_computation.7 | async-start | bytes 2162688 | tf_op jit(solution)/shard_map/reduce_scatter | solution.py:136
  1420.2 15.3 %all-to-all-start.1 = ((bf16[8,8,256]{2,1,0:T(8,128)(2,1)}), bf16[8,8,256]{2,1,0:T(8,128)(2,1)S(1)}, u32[]{:S(2)}, u32[]{:S(2)}) async-start(bf16[8,8,256]{2,1,0:T(8,128)(2,1)} %fusion.18), calls=%async_computation.2 | async-start | bytes 65536 | tf_op jit(solution)/shard_map/all_to_all | solution.py:141
  1437.6 17.3 %all-to-all-start.2 = ((bf16[32,2,1024]{2,1,0:T(2,128)(2,1)}), bf16[32,2,1024]{2,1,0:T(2,128)(2,1)S(1)}, u32[]{:S(2)}, u32[]{:S(2)}) async-start(bf16[32,2,1024]{2,1,0:T(2,128)(2,1)} %reshape.602), calls=%async_computation.3 | async-start | bytes 262144 | tf_op jit(solution)/shard_map/all_to_all | solution.py:148
Sparse Core Ops, SparseCore 0:
  9.5 27.0 all-gather.3
  748.7 80.8 all-gather.5
  977.0 216.5 reduce-scatter.6
  1197.8 219.9 reduce-scatter.4
where the time goes:
time: 1470 us; the launch traced here: 1460 us
  blocking collectives  631 us (43%)
  waiting for transfers between devices  515 us (35%)
  local copies, waits for them, and re-layouts  154 us (10%)
  starting transfers between devices  100 us (7%)
  other arithmetic  41 us (3%)
    all_gather x1, blocking collectives, on_device(): lax.all_gather(fresh_list.reshape(1, list_len), ('bal', 'uly'), axis=0, t...  606 us
    reduce_scatter x1, waiting for transfers between devices, on_device(): lax.psum_scatter(sums, 'bal', scatter_dimension=0, tiled=True)  224 us
    reduce_scatter x1, waiting for transfers between devices, on_device(): lax.psum_scatter(totals, 'bal', scatter_dimension=0, tiled=True)  213 us
    all_to_all x1, starting transfers between devices, on_device(): lax.all_to_all(outgoing, 'bal', split_axis=0, concat_axis=0, tiled=True)  83.8 us
    all_gather x1, waiting for transfers between devices, on_device(): everything = lax.all_gather(fresh, 'bal', axis=0, tiled=True)  60.9 us
    scatter x1, local copies, waits for them, and re-layouts, on_device(): value_block = value_block.at[spots].set(everything[:, :, 2], mode='drop')  59.4 us
    scatter x1, local copies, waits for them, and re-layouts, on_device(): key_block = key_block.at[spots].set(everything[:, :, 1], mode='drop')  59.4 us
  transfers between devices with their start and end apart: 7, of which 5 were waited for; matrix products, arithmetic and copies ran while one was open for 3% of the time, Pallas kernels for 0%

commit v1 on v0

v1 whole, which is shorter than its diff:
```python
import functools
import math

import jax
import jax.numpy as jnp
from jax import lax
from jax.experimental import pallas as pl
from jax.experimental.pallas import tpu as pltpu
from jax.sharding import PartitionSpec as P

HEAD_DIM = 128
BLOCK = 8
SIDE_X = 4
LANES = 128
MESH = pl.DeviceIdType.MESH
F32 = jnp.float32
BF16 = jnp.bfloat16


def normalize(values):
    return values * lax.rsqrt(jnp.mean(values * values, axis=-1, keepdims=True) + 1e-06)


def iota(shape, dim):
    return lax.broadcasted_iota(jnp.int32, shape, dim)


def dot(a, b):
    return jnp.dot(a, b, preferred_element_type=F32)


def dot_t(a, b):
    return lax.dot_general(a, b, (((1,), (1,)), ((), ())), preferred_element_type=F32)


def kernel(
    nx, nu, list_ref, hidden_ref, w_ref, gain_ref, ck_ref, cv_ref, out_ref,
    w_buf, lists, stage, out1, in1, xbuf, pkv, kv, qbuf, kvf, vaug, acc, rsout, rsin, ret_out, ret1,
    stage2, out2, in2,
    w_sem, list_s, list_r, p1_s, p1_r, z_s, z_r, f_s, kv_s, kv_r, q_s, q_r, kf_s, kf_r, rs_s, rs_r,
    ret_s, ret_r, back_s, back_r,
):
    b, u, c = lax.axis_index("bal"), lax.axis_index("uly"), lax.axis_index("cfg")
    nb, width = lists.shape[0], hidden_ref.shape[1]
    ny = nb // nx
    x, y = b // ny, b % ny
    toks = hidden_ref.shape[0]
    blocks = toks // BLOCK
    entries = list_ref.shape[0]
    keys = ck_ref.shape[0]
    half = nu * BLOCK
    pieces = width // LANES
    nh = 2 * nu
    other = 1 - c

    def bal_dev(k):
        return (lax.rem(b + k, nb), u, c)

    def x_dev(k):
        return (lax.rem(x + k, nx) * ny + y, u, c)

    def y_dev(k):
        return (x * ny + lax.rem(y + k, ny), u, c)

    def remote(src, dst, s, r, dev):
        return pltpu.make_async_remote_copy(
            src_ref=src, dst_ref=dst, send_sem=s, recv_sem=r, device_id=dev, device_id_type=MESH
        )

    def each(lo, hi, body):
        lax.fori_loop(lo, hi, lambda i, z: (body(i), z)[1], 0)

    w_copy = pltpu.make_async_copy(w_ref, w_buf, w_sem)
    w_copy.start()

    barrier = pltpu.get_barrier_semaphore()

    def greet_bal(k):
        pl.semaphore_signal(barrier, inc=1, device_id=bal_dev(k), device_id_type=MESH)

    def greet_z(k):
        flat = lax.rem(2 * u + c + k, nh)
        pl.semaphore_signal(
            barrier, inc=1, device_id=(b, flat // 2, lax.rem(flat, 2)), device_id_type=MESH
        )

    each(1, nb, greet_bal)
    each(1, nh, greet_z)

    for head in range(2):
        k_head = normalize(ck_ref[:, head * HEAD_DIM : (head + 1) * HEAD_DIM].astype(F32)).astype(BF16)
        v_head = cv_ref[:, head * HEAD_DIM : (head + 1) * HEAD_DIM]
        pkv[head, 0] = k_head
        pkv[head, 1] = v_head
    kv[x, c] = pkv[c]

    row = jnp.full((1, LANES), blocks, jnp.int32)
    lane = iota((1, LANES), 1)
    for j in range(entries):
        row = jnp.where(lane == j, list_ref[j], row)
    lists[b] = row

    pl.semaphore_wait(barrier, nb - 1 + nh - 1)

    def list_copy(k, slot):
        return remote(lists.at[b], lists.at[slot], list_s.at[k], list_r.at[slot], bal_dev(k))

    each(1, nb, lambda k: list_copy(k, b).start())

    partner_kv = remote(pkv.at[other], kv.at[x, c], kv_s.at[0], kv_r.at[x, c], (b, u, other))
    partner_kv.start()
    prev_x, next_x = lax.rem(x + nx - 1, nx), lax.rem(x + 1, nx)

    def ring(slot_x, branch, s, way):
        return remote(
            kv.at[slot_x, branch], kv.at[slot_x, branch], kv_s.at[s], kv_r.at[slot_x, branch], x_dev(way)
        )

    own_up, own_down = ring(x, c, 1, 1), ring(x, c, 2, nx - 1)
    own_up.start()
    own_down.start()

    each(1, nb, lambda k: list_copy(k, lax.rem(b + k, nb)).wait_recv())
    table = lists[...].reshape(nb, LANES)
    count = jnp.sum((table < blocks).astype(F32), axis=1, keepdims=True)
    sub_n, lane_n = iota((nb, nb), 0), iota((nb, nb), 1)
    start_row = jnp.sum(jnp.where(sub_n < lane_n, count, 0.0), axis=0, keepdims=True)
    count_row = jnp.sum(jnp.where(sub_n == lane_n, count, 0.0), axis=0, keepdims=True)
    start_col = jnp.sum(jnp.where(lane_n < sub_n, count_row, 0.0), axis=1, keepdims=True)
    my_start = jnp.sum(jnp.where(iota((1, nb), 1) == b, start_row, 0.0), axis=1, keepdims=True)
    my_count = jnp.sum(jnp.where(iota((1, nb), 1) == b, count_row, 0.0), axis=1, keepdims=True)
    start_row, count_row, start_col, count_col, my_start, my_count = (
        each_one.astype(jnp.int32) * BLOCK
        for each_one in (start_row, count_row, start_col, count, my_start, my_count)
    )

    dest = iota((nb, toks), 0)
    local = jnp.bitwise_and(dest - my_start, nb - 1)
    entry = local // BLOCK
    token = jnp.zeros((nb, toks), jnp.int32)
    for j in range(entries):
        token = jnp.where(entry == j, list_ref[j], token)
    token = token * BLOCK + local % BLOCK
    pick = (token == iota((nb, toks), 1)).astype(F32).astype(BF16)
    for j in range(pieces):
        stage[:, j, :] = dot(pick, hidden_ref[:, j * LANES : (j + 1) * LANES])
    out1[...] = stage[...].astype(BF16)

    def p1_copy(k, slot):
        to = lax.rem(b + k, nb)
        return remote(out1.at[to], in1.at[slot], p1_s.at[k], p1_r.at[slot], bal_dev(k))

    each(1, nb, lambda k: p1_copy(k, b).start())
    in1[b] = out1[b]

    remote(pkv.at[other], kv.at[x, other], kv_s.at[0], kv_r.at[x, other], (b, u, other)).wait_recv()
    their_up, their_down = ring(x, other, 3, 1), ring(x, other, 4, nx - 1)
    their_up.start()
    their_down.start()

    local_row = jnp.bitwise_and(b - start_row, nb - 1)
    slot_row = (start_row + local_row) // nb
    sel = (local_row < count_row) & (slot_row == iota((BLOCK, nb), 0))
    sel = sel.astype(F32).astype(BF16)
    near = (iota((BLOCK, nb), 1) == iota((BLOCK, nb), 0) * ny + y) & (iota((BLOCK, nb), 0) < nx)
    xbuf[c, u, :, width:] = dot(near.astype(F32).astype(BF16), table.astype(F32).astype(BF16)).astype(BF16)
    each(1, nb, lambda k: p1_copy(k, lax.rem(b + k, nb)).wait_recv())
    stage[...] = in1[...].astype(F32)
    for j in range(pieces):
        xbuf[c, u, :, j * LANES : (j + 1) * LANES] = dot(sel, stage[:, j, :].astype(BF16)).astype(BF16)

    def z_copy(k, slot):
        return remote(
            xbuf.at[c, u], xbuf.at[c, slot], z_s.at[k], z_r.at[c, slot], (b, lax.rem(u + k, nu), c)
        )

    def forward(branch, slot):
        return remote(
            xbuf.at[branch, slot], xbuf.at[branch, slot], f_s.at[slot], z_r.at[branch, slot], (b, u, other)
        )

    forward(c, u).start()
    order = []
    for k in range(1, nu // 2 + 1):
        order += [k] if 2 * k == nu else [k, nu - k]
    for k in order:
        z_copy(k, u).start()
    for k in order:
        slot = lax.rem(u + k, nu)
        z_copy(k, slot).wait_recv()
        forward(c, slot).start()

    ring(prev_x, c, 5, 1).wait_recv()
    on_up = ring(prev_x, c, 5, 1)
    on_up.start()
    ring(next_x, other, 6, nx - 1).wait_recv()
    on_down = ring(next_x, other, 6, nx - 1)
    on_down.start()

    each(0, nu, lambda k: forward(other, k).wait_recv())
    w_copy.wait()
    chunk = math.gcd(width, 1024)
    projected = jnp.zeros((2 * half, 3 * HEAD_DIM), F32)
    for j in range(0, width, chunk):
        rows = xbuf[:, :, :, j : j + chunk].astype(F32).reshape(2 * half, chunk).astype(BF16)
        projected = projected + dot(rows, w_buf[j : j + chunk, :])
    gains = gain_ref[pl.ds(c, 1), :]
    qbuf[y] = (normalize(projected[:, :HEAD_DIM]) * gains).astype(BF16)
    k_fresh = projected[:, HEAD_DIM : 2 * HEAD_DIM].astype(BF16).astype(F32)
    kvf[x, 0] = normalize(k_fresh).astype(BF16)
    kvf[x, 1] = projected[:, 2 * HEAD_DIM :].astype(BF16)

    def q_copy(k, slot):
        return remote(qbuf.at[y], qbuf.at[slot], q_s.at[k], q_r.at[slot], y_dev(k))

    def kf_copy(k, slot):
        return remote(kvf.at[x], kvf.at[slot], kf_s.at[k], kf_r.at[slot], x_dev(k))

    each(1, ny, lambda k: q_copy(k, y).start())
    each(1, nx, lambda k: kf_copy(k, x).start())

    for k in range(1, nx):
        slot = lax.rem(x + k, nx)
        if k == 1:
            ring(slot, c, 1, 1).wait_recv()
        elif k == nx - 1:
            ring(slot, other, 1, 1).wait_recv()
        else:
            ring(slot, c, 1, 1).wait_recv()
            ring(slot, other, 1, 1).wait_recv()
    span = nx * keys
    owner_hit = (iota((keys, nu), 0) // toks == iota((keys, nu), 1)).astype(F32).astype(BF16)
    block_hit = (iota((keys, LANES), 0) % toks) // BLOCK == iota((keys, LANES), 1)
    ones = jnp.ones((LANES, LANES), BF16)
    lane_u = iota((nu, LANES), 1).astype(F32)
    for branch in range(2):
        extra = xbuf[branch, :, :, width:].astype(F32)
        for k in range(nx):
            named = extra[:, k, :]
            hit = jnp.zeros((nu, LANES), F32)
            for j in range(entries):
                hit = hit + (named[:, j : j + 1] == lane_u).astype(F32)
            spread = jnp.where(block_hit, dot(owner_hit, hit.astype(BF16)), 0.0).astype(BF16)
            mask = 1.0 - dot(spread, ones)
            rows = pl.ds(k * keys, keys)
            vaug[branch, rows, :HEAD_DIM] = (kv[k, branch, 1].astype(F32) * mask).astype(BF16)
            vaug[branch, rows, HEAD_DIM:] = mask.astype(BF16)

    each(1, ny, lambda k: q_copy(k, lax.rem(y + k, ny)).wait_recv())
    each(1, nx, lambda k: kf_copy(k, lax.rem(x + k, nx)).wait_recv())
    factor = 1.0 / math.sqrt(HEAD_DIM)
    fresh_keys = nx * half

    for branch in range(2):
        mine = slice(branch * half, (branch + 1) * half)
        vaug[branch, span:, :HEAD_DIM] = kvf[:, 1, mine, :].reshape(fresh_keys, HEAD_DIM)
        vaug[branch, span:, HEAD_DIM:] = jnp.ones((fresh_keys, HEAD_DIM), BF16)
        queries = qbuf[:, mine, :].reshape(ny * half, HEAD_DIM)
        k_last = kvf[:, 0, mine, :].reshape(fresh_keys, HEAD_DIM)
        weights = jnp.exp(dot_t(queries, k_last) * factor).astype(BF16)
        acc[...] = dot(weights, vaug[branch, span:, :])

        def attend(k, branch=branch, queries=queries):
            weights = jnp.exp(dot_t(queries, kv[k, branch, 0]) * factor).astype(BF16)
            start = pl.multiple_of(k * keys, keys)
            acc[...] += dot(weights, vaug[branch, pl.ds(start, keys), :])

        each(0, nx, attend)
        rsout[:, mine, :] = acc[:, :HEAD_DIM].reshape(ny, half, HEAD_DIM).astype(BF16)
        totals = acc[:, HEAD_DIM:].reshape(ny, half, HEAD_DIM)
        place = iota((1, half, LANES), 2) == iota((1, half, LANES), 1) + branch * half
        flat = jnp.sum(jnp.where(place, totals, 0.0), axis=1, keepdims=True)
        all_totals = flat if branch == 0 else all_totals + flat
    coarse = all_totals.astype(BF16).astype(F32)
    tail = rsout.shape[1] - 2 * half
    tail_row = iota((ny, tail, LANES), 1)
    rsout[:, 2 * half :, :] = jnp.where(
        tail_row == 0, coarse, jnp.where(tail_row == 1, all_totals - coarse, 0.0)
    ).astype(BF16)

    def rs_copy(k, slot):
        to = lax.rem(y + k, ny)
        return remote(rsout.at[to], rsin.at[slot], rs_s.at[k], rs_r.at[slot], y_dev(k))

    each(1, ny, lambda k: rs_copy(k, y).start())
    rsin[y] = rsout[y]
    each(1, ny, lambda k: rs_copy(k, lax.rem(y + k, ny)).wait_recv())
    summed = jnp.sum(rsin[...].astype(F32), axis=0)
    total = summed[2 * half : 2 * half + 1, :] + summed[2 * half + 1 : 2 * half + 2, :]
    square = iota((2 * half, LANES), 0) == iota((2 * half, LANES), 1)
    total = jnp.sum(jnp.where(square, total, 0.0), axis=1, keepdims=True)
    attended = summed[: 2 * half, :] / total
    ret_out[...] = attended.reshape(nh, BLOCK, HEAD_DIM).astype(BF16)

    def ret_copy(k, slot):
        flat = lax.rem(2 * u + c + k, nh)
        to_u, to_c = flat // 2, lax.rem(flat, 2)
        return remote(
            ret_out.at[to_c * nu + to_u], ret1.at[slot], ret_s.at[k], ret_r.at[slot], (b, to_u, to_c)
        )

    each(1, nh, lambda k: ret_copy(k, 2 * u + c).start())
    ret1[2 * u + c] = ret_out[c * nu + u]
    slot_col = start_col + jnp.bitwise_and(b - start_col, nb - 1)
    give = (slot_col < start_col + count_col) & (slot_col // nb == iota((nb, BLOCK), 1))
    give = give.astype(F32).astype(BF16)
    each(1, nh, lambda k: ret_copy(k, lax.rem(2 * u + c + k, nh)).wait_recv())
    for h in range(nh):
        stage2[:, h, :] = dot(give, ret1[h])
    out2[...] = stage2[...].astype(BF16)

    def back_copy(k, slot):
        to = lax.rem(b + k, nb)
        return remote(out2.at[to], in2.at[slot], back_s.at[k], back_r.at[slot], bal_dev(k))

    each(1, nb, lambda k: back_copy(k, b).start())
    in2[b] = out2[b]
    spread_rows = iota((nb, nb), 0)
    final = (jnp.bitwise_and(my_start + spread_rows, nb - 1) == lane_n) & (spread_rows < my_count)
    final = final.astype(F32).astype(BF16)
    each(1, nb, lambda k: back_copy(k, lax.rem(b + k, nb)).wait_recv())
    stage2[...] = in2[...].astype(F32)
    for h in range(nh):
        out_ref[:, h * HEAD_DIM : (h + 1) * HEAD_DIM] = dot(final, stage2[:, h, :].astype(BF16)).astype(BF16)

    def sent_bal(k):
        list_copy(k, b).wait_send()
        p1_copy(k, b).wait_send()
        back_copy(k, b).wait_send()

    each(1, nb, sent_bal)
    each(1, nu, lambda k: z_copy(k, u).wait_send())
    each(0, nu, lambda k: forward(c, k).wait_send())
    for copy in (partner_kv, own_up, own_down, their_up, their_down, on_up, on_down):
        copy.wait_send()

    def sent_y(k):
        q_copy(k, y).wait_send()
        rs_copy(k, y).wait_send()

    each(1, ny, sent_y)
    each(1, nx, lambda k: kf_copy(k, x).wait_send())
    each(1, nh, lambda k: ret_copy(k, 2 * u + c).wait_send())


def on_device(hidden, w_qkv, q_gain, cache_k, cache_v, fresh_list):
    nb, nu = lax.axis_size("bal"), lax.axis_size("uly")
    nx = SIDE_X
    ny = nb // nx
    toks, width = hidden.shape[1:]
    keys = cache_k.shape[1]
    entries = fresh_list.shape[3]
    half = nu * BLOCK
    nh = 2 * nu
    pieces = width // LANES
    span = nx * (keys + half)
    vmem = pl.BlockSpec(memory_space=pltpu.VMEM)
    dma = pltpu.SemaphoreType.DMA
    out = pl.pallas_call(
        functools.partial(kernel, nx, nu),
        out_shape=jax.ShapeDtypeStruct((entries * BLOCK, nh * HEAD_DIM), BF16),
        in_specs=[
            pl.BlockSpec(memory_space=pltpu.SMEM),
            vmem,
            pl.BlockSpec(memory_space=pl.ANY),
            vmem,
            vmem,
            vmem,
        ],
        out_specs=vmem,
        scratch_shapes=[
            pltpu.VMEM(w_qkv.shape, BF16),
            pltpu.VMEM((nb, 1, LANES), jnp.int32),
            pltpu.VMEM((nb, pieces, LANES), F32),
            pltpu.VMEM((nb, pieces, LANES), BF16),
            pltpu.VMEM((nb, pieces, LANES), BF16),
            pltpu.VMEM((2, nu, BLOCK, width + LANES), BF16),
            pltpu.VMEM((2, 2, keys, HEAD_DIM), BF16),
            pltpu.VMEM((nx, 2, 2, keys, HEAD_DIM), BF16),
            pltpu.VMEM((ny, 2 * half, HEAD_DIM), BF16),
            pltpu.VMEM((nx, 2, 2 * half, HEAD_DIM), BF16),
            pltpu.VMEM((2, span, 2 * HEAD_DIM), BF16),
            pltpu.VMEM((ny * half, 2 * HEAD_DIM), F32),
            pltpu.VMEM((ny, 2 * half + 16, HEAD_DIM), BF16),
            pltpu.VMEM((ny, 2 * half + 16, HEAD_DIM), BF16),
            pltpu.VMEM((nh, BLOCK, HEAD_DIM), BF16),
            pltpu.VMEM((nh, BLOCK, HEAD_DIM), BF16),
            pltpu.VMEM((nb, nh, HEAD_DIM), F32),
            pltpu.VMEM((nb, nh, HEAD_DIM), BF16),
            pltpu.VMEM((nb, nh, HEAD_DIM), BF16),
            dma,
            dma((nb,)), dma((nb,)),
            dma((nb,)), dma((nb,)),
            dma((nu,)), dma((2, nu)),
            dma((nu,)),
            dma((7,)), dma((nx, 2)),
            dma((ny,)), dma((ny,)),
            dma((nx,)), dma((nx,)),
            dma((ny,)), dma((ny,)),
            dma((nh,)), dma((nh,)),
            dma((nb,)), dma((nb,)),
        ],
        compiler_params=pltpu.CompilerParams(
            collective_id=0, has_side_effects=True, vmem_limit_bytes=48 * 1024 * 1024
        ),
    )(
        fresh_list.reshape(entries),
        hidden.reshape(toks, width),
        w_qkv,
        q_gain.reshape(2, HEAD_DIM),
        cache_k.reshape(keys, 2 * HEAD_DIM),
        cache_v.reshape(keys, 2 * HEAD_DIM),
    )
    return out.reshape(1, 1, 1, entries * BLOCK, nh * HEAD_DIM)


def solution(mesh):
    in_specs = (
        P("cfg", ("bal", "uly"), None),
        P(None, ("uly", "cfg")),
        P("uly"),
        P("cfg", "bal", "uly"),
        P("cfg", "bal", "uly"),
        P("cfg", "bal", "uly", None),
    )
    out_specs = P("cfg", "bal", "uly", None, None)
    return jax.shard_map(
        on_device, mesh=mesh, in_specs=in_specs, out_specs=out_specs, check_vma=False
    )
```

time: 1470 us -> 87.9 us (0.06)
  the two profiles are of different devices: /device:TPU:2 before, /device:TPU:8 now
where the time goes in v1:
time: 87.9 us; the launch traced here: 87.2 us
  Pallas kernels  80.6 us (92%)
  local copies, waits for them, and re-layouts  6.55 us (7%)
    pallas_call x1, Pallas kernels, on_device(): pl.pallas_call(functools.partial(kernel, nx, nu), out_shape=jax.ShapeDtyp...  80.6 us
    unnamed x13, local copies, waits for them, and re-layouts  6.55 us

profile of v1, /device:TPU:8, one launch (start us, length us, event | category | flops | bytes accessed | tf_op | source)
XLA Modules:
  0.0 87.2 jit_solution(6125950422385005031)
XLA Ops:
  0.0 0.0 copy-start
  0.0 1.7 %copy-done = bf16[3072,384]{1,0:T(8,128)(2,1)S(1)} copy-done((bf16[3072,384]{1,0:T(8,128)(2,1)S(1)}, bf16[3072,384]{1,0:T(8,128)(2,1)}, u32[]{:S(2)}) %copy-start) | copy-done | bytes 2359320
  1.7 0.0 copy-start.1
  1.7 1.0 %copy-done.1 = bf16[1,64,3072]{2,1,0:T(8,128)(2,1)S(1)} copy-done((bf16[1,64,3072]{2,1,0:T(8,128)(2,1)S(1)}, bf16[1,64,3072]{2,1,0:T(8,128)(2,1)}, u32[]{:S(2)}) %copy-start.1) | copy-done | bytes 393240
  2.7 0.0 copy-start.2
  2.7 0.9 %copy-done.2 = bf16[1,512,256]{2,1,0:T(8,128)(2,1)S(1)} copy-done((bf16[1,512,256]{2,1,0:T(8,128)(2,1)S(1)}, bf16[1,512,256]{2,1,0:T(8,128)(2,1)}, u32[]{:S(2)}) %copy-start.2) | copy-done | bytes 262168
  3.6 0.0 copy-start.3
  3.6 0.9 %copy-done.3 = bf16[1,512,256]{2,1,0:T(8,128)(2,1)S(1)} copy-done((bf16[1,512,256]{2,1,0:T(8,128)(2,1)S(1)}, bf16[1,512,256]{2,1,0:T(8,128)(2,1)}, u32[]{:S(2)}) %copy-start.3) | copy-done | bytes 262168
  4.6 0.0 copy-start.4
  4.6 0.7 copy-done.4
  5.2 0.0 copy-start.5
  5.2 0.7 copy-done.5
  5.9 80.6 %shard_map.64 = bf16[32,2048]{1,0:T(8,128)(2,1)S(1)} custom-call(s32[4]{0:T(128)S(1)} %bitcast.11, bf16[64,3072]{1,0:T(8,128)(2,1)S(1)} %bitcast.7, bf16[3072,384]{1,0:T(8,128)(2,1)S(1)} %copy-done, f32[2,128]{1,0:T(2,128)S(1)} %bitcast.10, bf16[512,256]{1,0:T(8,128)(2,1)S(1)} %bitcast.8, bf16[512,256]{1,0:T(8,128)(2,1)S(1)} %bitcast.9), custom_call_target="tpu_custom_call" | custom-call | tf_op jit(solution)/shard_map/pallas_call | solution.py:359
  86.5 0.7 copy.8
Async XLA Ops:
  0.0 1.7 %copy-start = (bf16[3072,384]{1,0:T(8,128)(2,1)S(1)}, bf16[3072,384]{1,0:T(8,128)(2,1)}, u32[]{:S(2)}) copy-start(bf16[3072,384]{1,0:T(8,128)(2,1)} %w_ref.1) | copy-start | bytes 7077892
  1.7 1.0 %copy-start.1 = (bf16[1,64,3072]{2,1,0:T(8,128)(2,1)S(1)}, bf16[1,64,3072]{2,1,0:T(8,128)(2,1)}, u32[]{:S(2)}) copy-start(bf16[1,64,3072]{2,1,0:T(8,128)(2,1)} %param.6) | copy-start | bytes 1179652
  2.7 0.9 %copy-start.2 = (bf16[1,512,256]{2,1,0:T(8,128)(2,1)S(1)}, bf16[1,512,256]{2,1,0:T(8,128)(2,1)}, u32[]{:S(2)}) copy-start(bf16[1,512,256]{2,1,0:T(8,128)(2,1)} %param.9) | copy-start | bytes 786436
  3.6 0.9 %copy-start.3 = (bf16[1,512,256]{2,1,0:T(8,128)(2,1)S(1)}, bf16[1,512,256]{2,1,0:T(8,128)(2,1)}, u32[]{:S(2)}) copy-start(bf16[1,512,256]{2,1,0:T(8,128)(2,1)} %param.10) | copy-start | bytes 786436
  4.6 0.7 copy-start.4
  5.2 0.7 copy-start.5

commit v2 on v1

v2 whole, which is shorter than its diff:
```python
import functools
import math

import jax
import jax.numpy as jnp
from jax import lax
from jax.experimental import pallas as pl
from jax.experimental.pallas import tpu as pltpu
from jax.sharding import PartitionSpec as P

HEAD_DIM = 128
BLOCK = 8
SIDE_X = 4
LANES = 128
MESH = pl.DeviceIdType.MESH
F32 = jnp.float32
BF16 = jnp.bfloat16


def normalize(values):
    return values * lax.rsqrt(jnp.mean(values * values, axis=-1, keepdims=True) + 1e-06)


def iota(shape, dim):
    return lax.broadcasted_iota(jnp.int32, shape, dim)


def dot(a, b):
    return jnp.dot(a, b, preferred_element_type=F32)


def dot_t(a, b):
    return lax.dot_general(a, b, (((1,), (1,)), ((), ())), preferred_element_type=F32)


def kernel(
    nx, nu, list_in, hidden_in, w_in, gain_in, ck_in, cv_in, out_ref,
    list_ref, hidden_ref, w_buf, gain_ref, ck_ref, cv_ref, lists, stage, out1, in1, xbuf, kv, qbuf, kvf,
    vaug, rsout, rsin, ret_out, ret1, stage2, out2, in2,
    in_sem, w_s, w_r, list_s, list_r, p1_s, p1_r, z_s, z_r, kv_s, kv_r, q_s, q_r, kf_s, kf_r, rs_s, rs_r,
    ret_s, ret_r, back_s, back_r,
):
    b, u, c = lax.axis_index("bal"), lax.axis_index("uly"), lax.axis_index("cfg")
    nb, width = lists.shape[0], hidden_ref.shape[1]
    ny = nb // nx
    x, y = b // ny, b % ny
    toks = hidden_ref.shape[0]
    blocks = toks // BLOCK
    entries = list_ref.shape[0]
    keys = ck_ref.shape[0]
    half = nu * BLOCK
    pieces = width // LANES
    nh = 2 * nu
    other = 1 - c

    def bal_dev(k):
        return (lax.rem(b + k, nb), u, c)

    def x_dev(k):
        return (lax.rem(x + k, nx) * ny + y, u, c)

    def y_dev(k):
        return (x * ny + lax.rem(y + k, ny), u, c)

    def z_dev(k):
        return (b, lax.rem(u + k, nu), c)

    def remote(src, dst, s, r, dev):
        return pltpu.make_async_remote_copy(
            src_ref=src, dst_ref=dst, send_sem=s, recv_sem=r, device_id=dev, device_id_type=MESH
        )

    def each(lo, hi, body):
        lax.fori_loop(lo, hi, lambda i, z: (body(i), z)[1], 0)

    pairs = (
        (list_in, list_ref),
        (ck_in, ck_ref),
        (cv_in, cv_ref),
        (w_in, w_buf.at[c]),
        (hidden_in, hidden_ref),
        (gain_in, gain_ref),
    )
    loads = tuple(
        pltpu.make_async_copy(src, dst, in_sem.at[i]) for i, (src, dst) in enumerate(pairs)
    )
    for load in loads:
        load.start()
    list_load, k_load, v_load, w_load, hidden_load, gain_load = loads
    cleanup = []

    barrier = pltpu.get_barrier_semaphore()

    def greet(dev):
        pl.semaphore_signal(barrier, inc=1, device_id=dev, device_id_type=MESH)

    each(1, nb, lambda k: greet(bal_dev(k)))
    each(1, nu, lambda k: greet(z_dev(k)))
    greet((b, u, other))

    list_load.wait()
    my_rows = 0
    for j in range(entries):
        my_rows = my_rows + jnp.where(list_ref[j] < blocks, BLOCK, 0)
    lane = iota((1, LANES), 1)
    row = jnp.zeros((1, LANES), jnp.int32) + my_rows
    for j in range(entries):
        row = jnp.where(lane == LANES - entries + j, list_ref[j], row)
    lists[b] = row

    k_load.wait()
    v_load.wait()
    for head in range(2):
        columns = slice(head * HEAD_DIM, (head + 1) * HEAD_DIM)
        kv[x, head, 0] = normalize(ck_ref[:, columns].astype(F32)).astype(BF16)
        kv[x, head, 1] = cv_ref[:, columns]
    w_load.wait()
    hidden_load.wait()

    pl.semaphore_wait(barrier, nb - 1 + nu - 1 + 1)

    def list_copy(k, slot):
        return remote(lists.at[b], lists.at[slot], list_s.at[k], list_r.at[slot], bal_dev(k))

    each(1, nb, lambda k: list_copy(k, b).start())
    cleanup.append(lambda: each(1, nb, lambda k: list_copy(k, b).wait_send()))

    prev_x, next_x = lax.rem(x + nx - 1, nx), lax.rem(x + 1, nx)

    def ring(slot_x, s, way):
        return remote(kv.at[slot_x], kv.at[slot_x], kv_s.at[s], kv_r.at[slot_x], x_dev(way))

    def ring_head(slot_x, head, s, way):
        part = kv.at[slot_x, head]
        return remote(part, part, kv_s.at[s], kv_r.at[nx + head], x_dev(way))

    own_up, own_down = ring(x, 0, 1), ring(x, 1, nx - 1)
    own_up.start()
    own_down.start()
    cleanup.extend((own_up.wait_send, own_down.wait_send))
    w_out = remote(w_buf.at[c], w_buf.at[c], w_s, w_r, (b, u, other))
    w_out.start()
    cleanup.append(w_out.wait_send)

    dest = iota((nb, toks), 0)
    each(1, nb, lambda k: list_copy(k, lax.rem(b + k, nb)).wait_recv())
    table = lists[...].reshape(nb, LANES).astype(F32)
    sub_n, lane_n = iota((nb, nb), 0), iota((nb, nb), 1)
    my_start = jnp.sum(jnp.where(iota((nb, LANES), 0) < b, table, 0.0), axis=0, keepdims=True)
    my_start = my_start.astype(jnp.int32)
    local = jnp.bitwise_and(dest - my_start[:, :toks], nb - 1)
    entry = local // BLOCK
    token = jnp.zeros((nb, toks), jnp.int32)
    for j in range(entries):
        token = jnp.where(entry == j, list_ref[j], token)
    token = token * BLOCK + local % BLOCK
    pick = (token == iota((nb, toks), 1)).astype(F32).astype(BF16)
    for j in range(pieces):
        stage[:, j, :] = dot(pick, hidden_ref[:, j * LANES : (j + 1) * LANES])
    out1[...] = stage[...].astype(BF16)

    def p1_copy(k, slot):
        to = lax.rem(b + k, nb)
        return remote(out1.at[to], in1.at[slot], p1_s.at[k], p1_r.at[slot], bal_dev(k))

    each(1, nb, lambda k: p1_copy(k, b).start())
    cleanup.append(lambda: each(1, nb, lambda k: p1_copy(k, b).wait_send()))
    in1[b] = out1[b]

    counts = table[:, :nb]
    start_row = jnp.sum(jnp.where(sub_n < lane_n, counts, 0.0), axis=0, keepdims=True).astype(jnp.int32)
    count_row = jnp.sum(jnp.where(sub_n == lane_n, counts, 0.0), axis=0, keepdims=True)
    start_col = jnp.sum(jnp.where(lane_n < sub_n, count_row, 0.0), axis=1, keepdims=True).astype(jnp.int32)
    count_row = count_row.astype(jnp.int32)
    count_col = counts[:, :BLOCK].astype(jnp.int32)
    local_row = jnp.bitwise_and(b - start_row, nb - 1)
    slot_row = (start_row + local_row) // nb
    sel = (local_row < count_row) & (slot_row == iota((BLOCK, nb), 0))
    sel = sel.astype(F32).astype(BF16)
    near = (iota((BLOCK, nb), 1) == iota((BLOCK, nb), 0) * ny + y) & (iota((BLOCK, nb), 0) < nx)
    xbuf[u, :, width:] = dot(near.astype(F32).astype(BF16), table.astype(BF16)).astype(BF16)
    each(1, nb, lambda k: p1_copy(k, lax.rem(b + k, nb)).wait_recv())
    stage[...] = in1[...].astype(F32)
    for j in range(pieces):
        xbuf[u, :, j * LANES : (j + 1) * LANES] = dot(sel, stage[:, j, :].astype(BF16)).astype(BF16)

    def z_copy(k, slot):
        return remote(xbuf.at[u], xbuf.at[slot], z_s.at[k], z_r.at[slot], z_dev(k))

    order = []
    for k in range(nu // 2, 0, -1):
        order += [k] if 2 * k == nu else [k, nu - k]
    for k in order:
        z_copy(k, u).start()
    cleanup.append(lambda: each(1, nu, lambda k: z_copy(k, u).wait_send()))

    ring(prev_x, 0, 1).wait_recv()
    ring(next_x, 0, 1).wait_recv()
    on_up, on_down = ring_head(prev_x, 0, 2, 1), ring_head(next_x, 1, 3, nx - 1)
    on_up.start()
    on_down.start()
    cleanup.extend((on_up.wait_send, on_down.wait_send))
    w_out.wait_recv()
    gain_load.wait()

    each(1, nu, lambda k: z_copy(k, lax.rem(u + k, nu)).wait_recv())
    chunk = math.gcd(width, 1024)
    projected = [jnp.zeros((half, 3 * HEAD_DIM), F32)] * 2
    for j in range(0, width, chunk):
        rows = xbuf[:, :, j : j + chunk].astype(F32).reshape(half, chunk).astype(BF16)
        projected = [projected[h] + dot(rows, w_buf[h, j : j + chunk, :]) for h in range(2)]
    for h in range(2):
        mine = slice(h * half, (h + 1) * half)
        query = normalize(projected[h][:, :HEAD_DIM]) * gain_ref[h : h + 1, :]
        qbuf[y, mine, :] = query.astype(BF16)

    def q_copy(k, slot):
        return remote(qbuf.at[y], qbuf.at[slot], q_s.at[k], q_r.at[slot], y_dev(k))

    def kf_copy(k, slot):
        return remote(kvf.at[x], kvf.at[slot], kf_s.at[k], kf_r.at[slot], x_dev(k))

    for k in range(1, ny // 2 + 1):
        for way in [k] if 2 * k == ny else [k, ny - k]:
            q_copy(way, y).start()
    for h in range(2):
        mine = slice(h * half, (h + 1) * half)
        k_fresh = projected[h][:, HEAD_DIM : 2 * HEAD_DIM].astype(BF16).astype(F32)
        kvf[x, 0, mine, :] = normalize(k_fresh).astype(BF16)
        kvf[x, 1, mine, :] = projected[h][:, 2 * HEAD_DIM :].astype(BF16)
    each(1, nx, lambda k: kf_copy(k, x).start())
    cleanup.append(lambda: each(1, ny, lambda k: q_copy(k, y).wait_send()))
    cleanup.append(lambda: each(1, nx, lambda k: kf_copy(k, x).wait_send()))

    far_x = lax.rem(x + nx // 2, nx)
    ring_head(far_x, 0, 2, 1).wait_recv()
    ring_head(far_x, 1, 3, nx - 1).wait_recv()
    span = nx * keys
    owner_hit = (iota((keys, nu), 0) // toks == iota((keys, nu), 1)).astype(F32).astype(BF16)
    block_hit = (iota((keys, LANES), 0) % toks) // BLOCK == iota((keys, LANES), 1)
    ones = jnp.ones((LANES, LANES), BF16)
    lane_u = iota((nu, LANES), 1).astype(F32)
    extra = xbuf[:, :, width:].astype(F32)
    for k in range(nx):
        named = extra[:, k, :]
        hit = jnp.zeros((nu, LANES), F32)
        for j in range(LANES - entries, LANES):
            hit = hit + (named[:, j : j + 1] == lane_u).astype(F32)
        spread = jnp.where(block_hit, dot(owner_hit, hit.astype(BF16)), 0.0).astype(BF16)
        mask = 1.0 - dot(spread, ones)
        rows = pl.ds(k * keys, keys)
        for h in range(2):
            vaug[h, rows, :HEAD_DIM] = (kv[k, h, 1].astype(F32) * mask).astype(BF16)
            vaug[h, rows, HEAD_DIM:] = mask.astype(BF16)

    each(1, nx, lambda k: kf_copy(k, lax.rem(x + k, nx)).wait_recv())
    fresh_keys = nx * half
    for h in range(2):
        mine = slice(h * half, (h + 1) * half)
        vaug[h, span:, :HEAD_DIM] = kvf[:, 1, mine, :].reshape(fresh_keys, HEAD_DIM)
        vaug[h, span:, HEAD_DIM:] = jnp.ones((fresh_keys, HEAD_DIM), BF16)
    factor = 1.0 / math.sqrt(HEAD_DIM)

    def weigh(queries, some_keys):
        return jnp.exp(dot_t(queries, some_keys) * factor).astype(BF16)

    def rs_copy(k, slot):
        to = lax.rem(y + k, ny)
        return remote(rsout.at[to], rsin.at[slot], rs_s.at[k], rs_r.at[slot], y_dev(k))

    def attend(i):
        way_a, way_b = lax.rem(ny - i, ny), i + 1
        slot_a, slot_b = lax.rem(y + way_a, ny), lax.rem(y + way_b, ny)

        @pl.when(i > 0)
        def _():
            q_copy(way_a, slot_a).wait_recv()

        q_copy(way_b, slot_b).wait_recv()
        flat_a = jnp.zeros((1, LANES), F32)
        flat_b = jnp.zeros((1, LANES), F32)
        for h in range(2):
            mine = slice(h * half, (h + 1) * half)
            queries = jnp.concatenate([qbuf[slot_a, mine, :], qbuf[slot_b, mine, :]], axis=0)
            k_last = kvf[:, 0, mine, :].reshape(fresh_keys, HEAD_DIM)
            got = dot(weigh(queries, k_last), vaug[h, span:, :])
            for k in range(nx):
                got = got + dot(weigh(queries, kv[k, h, 0]), vaug[h, k * keys : (k + 1) * keys, :])
            rsout[slot_a, mine, :] = got[:half, :HEAD_DIM].astype(BF16)
            rsout[slot_b, mine, :] = got[half:, :HEAD_DIM].astype(BF16)
            place = iota((half, LANES), 1) == iota((half, LANES), 0) + h * half
            flat_a = flat_a + jnp.sum(jnp.where(place, got[:half, HEAD_DIM:], 0.0), axis=0, keepdims=True)
            flat_b = flat_b + jnp.sum(jnp.where(place, got[half:, HEAD_DIM:], 0.0), axis=0, keepdims=True)
        tail = rsout.shape[1] - 2 * half
        tail_row = iota((tail, LANES), 0)
        for slot, flat in ((slot_a, flat_a), (slot_b, flat_b)):
            coarse = flat.astype(BF16).astype(F32)
            rest = jnp.where(tail_row == 1, flat - coarse, 0.0)
            rsout[slot, 2 * half :, :] = jnp.where(tail_row == 0, coarse, rest).astype(BF16)

        @pl.when(i > 0)
        def _():
            rs_copy(way_a, y).start()

        rs_copy(way_b, y).start()

    each(0, ny // 2, attend)
    cleanup.append(lambda: each(1, ny, lambda k: rs_copy(k, y).wait_send()))
    rsin[y] = rsout[y]

    each(1, ny, lambda k: rs_copy(k, lax.rem(y + k, ny)).wait_recv())
    summed = jnp.sum(rsin[...].astype(F32), axis=0)
    total = summed[2 * half : 2 * half + 1, :] + summed[2 * half + 1 : 2 * half + 2, :]
    square = iota((2 * half, LANES), 0) == iota((2 * half, LANES), 1)
    total = jnp.sum(jnp.where(square, total, 0.0), axis=1, keepdims=True)
    attended = summed[: 2 * half, :] / total
    for h in range(2):
        rows = attended[h * half : (h + 1) * half, :]
        ret_out[:, h] = rows.reshape(nu, BLOCK, HEAD_DIM).astype(BF16)

    def ret_copy(k, slot):
        to = lax.rem(u + k, nu)
        return remote(ret_out.at[to], ret1.at[slot], ret_s.at[k], ret_r.at[slot], z_dev(k))

    each(1, nu, lambda k: ret_copy(k, u).start())
    cleanup.append(lambda: each(1, nu, lambda k: ret_copy(k, u).wait_send()))
    ret1[u] = ret_out[u]
    slot_col = start_col + jnp.bitwise_and(b - start_col, nb - 1)
    give = (slot_col < start_col + count_col) & (slot_col // nb == iota((nb, BLOCK), 1))
    give = give.astype(F32).astype(BF16)
    each(1, nu, lambda k: ret_copy(k, lax.rem(u + k, nu)).wait_recv())
    for h in range(nh):
        stage2[:, h, :] = dot(give, ret1[h // 2, h % 2])
    out2[...] = stage2[...].astype(BF16)

    def back_copy(k, slot):
        to = lax.rem(b + k, nb)
        return remote(out2.at[to], in2.at[slot], back_s.at[k], back_r.at[slot], bal_dev(k))

    each(1, nb, lambda k: back_copy(k, b).start())
    cleanup.append(lambda: each(1, nb, lambda k: back_copy(k, b).wait_send()))
    in2[b] = out2[b]
    spread_rows = iota((nb, nb), 0)
    final = jnp.bitwise_and(my_start[:, :nb] + spread_rows, nb - 1) == lane_n
    final = (final & (spread_rows < my_rows)).astype(F32).astype(BF16)
    each(1, nb, lambda k: back_copy(k, lax.rem(b + k, nb)).wait_recv())
    stage2[...] = in2[...].astype(F32)
    for h in range(nh):
        out_ref[:, h * HEAD_DIM : (h + 1) * HEAD_DIM] = dot(final, stage2[:, h, :].astype(BF16)).astype(BF16)

    for finish in cleanup:
        finish()


def on_device(hidden, w_qkv, q_gain, cache_k, cache_v, fresh_list):
    nb, nu = lax.axis_size("bal"), lax.axis_size("uly")
    nx = SIDE_X
    ny = nb // nx
    toks, width = hidden.shape[1:]
    keys = cache_k.shape[1]
    entries = fresh_list.shape[3]
    half = nu * BLOCK
    nh = 2 * nu
    pieces = width // LANES
    span = nx * (keys + half)
    vmem = pl.BlockSpec(memory_space=pltpu.VMEM)
    dma = pltpu.SemaphoreType.DMA
    out = pl.pallas_call(
        functools.partial(kernel, nx, nu),
        out_shape=jax.ShapeDtypeStruct((entries * BLOCK, nh * HEAD_DIM), BF16),
        in_specs=[
            *[pl.BlockSpec(memory_space=pltpu.HBM)] * 6,
        ],
        out_specs=vmem,
        scratch_shapes=[
            pltpu.SMEM((entries,), jnp.int32),
            pltpu.VMEM((toks, width), BF16),
            pltpu.VMEM((2, *w_qkv.shape), BF16),
            pltpu.VMEM((2, HEAD_DIM), F32),
            pltpu.VMEM((keys, 2 * HEAD_DIM), BF16),
            pltpu.VMEM((keys, 2 * HEAD_DIM), BF16),
            pltpu.VMEM((nb, 1, LANES), jnp.int32),
            pltpu.VMEM((nb, pieces, LANES), F32),
            pltpu.VMEM((nb, pieces, LANES), BF16),
            pltpu.VMEM((nb, pieces, LANES), BF16),
            pltpu.VMEM((nu, BLOCK, width + LANES), BF16),
            pltpu.VMEM((nx, 2, 2, keys, HEAD_DIM), BF16),
            pltpu.VMEM((ny, 2 * half, HEAD_DIM), BF16),
            pltpu.VMEM((nx, 2, 2 * half, HEAD_DIM), BF16),
            pltpu.VMEM((2, span, 2 * HEAD_DIM), BF16),
            pltpu.VMEM((ny, 2 * half + 16, HEAD_DIM), BF16),
            pltpu.VMEM((ny, 2 * half + 16, HEAD_DIM), BF16),
            pltpu.VMEM((nu, 2, BLOCK, HEAD_DIM), BF16),
            pltpu.VMEM((nu, 2, BLOCK, HEAD_DIM), BF16),
            pltpu.VMEM((nb, nh, HEAD_DIM), F32),
            pltpu.VMEM((nb, nh, HEAD_DIM), BF16),
            pltpu.VMEM((nb, nh, HEAD_DIM), BF16),
            dma((6,)),
            dma, dma,
            dma((nb,)), dma((nb,)),
            dma((nb,)), dma((nb,)),
            dma((nu,)), dma((nu,)),
            dma((4,)), dma((nx + 2,)),
            dma((ny,)), dma((ny,)),
            dma((nx,)), dma((nx,)),
            dma((ny,)), dma((ny,)),
            dma((nu,)), dma((nu,)),
            dma((nb,)), dma((nb,)),
        ],
        compiler_params=pltpu.CompilerParams(
            collective_id=0, has_side_effects=True, vmem_limit_bytes=63 * 1024 * 1024
        ),
    )(
        fresh_list.reshape(entries),
        hidden.reshape(toks, width),
        w_qkv,
        q_gain.reshape(2, HEAD_DIM),
        cache_k.reshape(keys, 2 * HEAD_DIM),
        cache_v.reshape(keys, 2 * HEAD_DIM),
    )
    return out.reshape(1, 1, 1, entries * BLOCK, nh * HEAD_DIM)


def solution(mesh):
    in_specs = (
        P("cfg", ("bal", "uly"), None),
        P(None, ("uly", "cfg")),
        P("uly"),
        P("cfg", "bal", "uly"),
        P("cfg", "bal", "uly"),
        P("cfg", "bal", "uly", None),
    )
    out_specs = P("cfg", "bal", "uly", None, None)
    return jax.shard_map(
        on_device, mesh=mesh, in_specs=in_specs, out_specs=out_specs, check_vma=False
    )
```

time: 87.9 us -> 75.6 us (0.86)
  Pallas kernels: 80.6 us -> 73.9 us
  local copies, waits for them, and re-layouts: 6.55 us -> 1.57 us
    pallas_call x1, Pallas kernels: 80.6 us -> 73.9 us  [on_device(): pl.pallas_call(functools.partial(kernel, nx, nu), out_shape=jax.ShapeDtyp...]
    unnamed x13 -> x1, local copies, waits for them, and re-layouts: 6.55 us -> 1.57 us
where the time goes in v2:
time: 75.6 us; the launch traced here: 75.4 us
  Pallas kernels  73.9 us (98%)
  local copies, waits for them, and re-layouts  1.57 us (2%)
    pallas_call x1, Pallas kernels, on_device(): pl.pallas_call(functools.partial(kernel, nx, nu), out_shape=jax.ShapeDtyp...  73.9 us
    unnamed x1, local copies, waits for them, and re-layouts  1.57 us

profile of v2, /device:TPU:8, one launch (start us, length us, event | category | flops | bytes accessed | tf_op | source)
XLA Modules:
  0.0 75.4 jit_solution(3099980577543947070)
XLA Ops:
  0.0 73.9 %shard_map.64 = bf16[32,2048]{1,0:T(8,128)(2,1)} custom-call(s32[4]{0:T(128)} %bitcast.11, bf16[64,3072]{1,0:T(8,128)(2,1)} %bitcast.7, bf16[3072,384]{1,0:T(8,128)(2,1)} %w_in.1, f32[2,128]{1,0:T(2,128)} %bitcast.10, bf16[512,256]{1,0:T(8,128)(2,1)} %bitcast.8, bf16[512,256]{1,0:T(8,128)(2,1)} %bitcast.9), custom_call_target="tpu_custom_call" | custom-call | tf_op jit(solution)/shard_map/pallas_call | solution.py:368
  73.9 1.6 %copy.8 = bf16[1,1,1,32,2048]{4,3,2,1,0:T(8,128)(2,1)} copy(bf16[1,1,1,32,2048]{4,3,2,1,0:T(8,128)(2,1)} %bitcast.6) | data formatting | bytes 262144

commit v3 on v2

--- a/solution.py
+++ b/solution.py
@@ -35,9 +35,9 @@
 
 def kernel(
     nx, nu, list_in, hidden_in, w_in, gain_in, ck_in, cv_in, out_ref,
-    list_ref, hidden_ref, w_buf, gain_ref, ck_ref, cv_ref, lists, stage, out1, in1, xbuf, kv, qbuf, kvf,
+    list_ref, hidden_ref, w_buf, gain_ref, ck_ref, cv_ref, lists, named, stage, out1, in1, outx, inx, xbuf, kv, qbuf, kvf,
     vaug, rsout, rsin, ret_out, ret1, stage2, out2, in2,
-    in_sem, w_s, w_r, list_s, list_r, p1_s, p1_r, z_s, z_r, kv_s, kv_r, q_s, q_r, kf_s, kf_r, rs_s, rs_r,
+    in_sem, w_s, w_r, list_s, list_r, name_s, name_r, p1_s, p1_r, px_s, px_r, z_s, z_r, kv_s, kv_r, q_s, q_r, kf_s, kf_r, rs_s, rs_r,
     ret_s, ret_r, back_s, back_r,
 ):
     b, u, c = lax.axis_index("bal"), lax.axis_index("uly"), lax.axis_index("cfg")
@@ -53,8 +53,21 @@
     nh = 2 * nu
     other = 1 - c
 
+    def farthest(j, n):
+        step = (j + 1) // 2
+        return lax.rem(n // 2 + n + jnp.where(lax.rem(j, 2) == 1, step, -step), n)
+
+    def x_of(k):
+        return lax.rem(x + farthest(k - 1, nx), nx)
+
+    def y_of(k):
+        return lax.rem(y + farthest(k - 1, ny), ny)
+
+    def bal_of(k):
+        return x_of(lax.rem(k - 1, nx) + 1) * ny + y_of((k - 1) // nx + 1)
+
     def bal_dev(k):
-        return (lax.rem(b + k, nb), u, c)
+        return (bal_of(k), u, c)
 
     def x_dev(k):
         return (lax.rem(x + k, nx) * ny + y, u, c)
@@ -99,14 +112,24 @@
     greet((b, u, other))
 
     list_load.wait()
-    my_rows = 0
+    my_blocks = 0
     for j in range(entries):
-        my_rows = my_rows + jnp.where(list_ref[j] < blocks, BLOCK, 0)
+        my_blocks = my_blocks + jnp.where(list_ref[j] < blocks, 1, 0)
     lane = iota((1, LANES), 1)
-    row = jnp.zeros((1, LANES), jnp.int32) + my_rows
+    row = jnp.zeros((1, LANES), jnp.int32) + my_blocks
     for j in range(entries):
         row = jnp.where(lane == LANES - entries + j, list_ref[j], row)
     lists[b] = row
+
+    hidden_load.wait()
+    token = jnp.zeros((nb, toks), jnp.int32)
+    for j in range(entries):
+        token = jnp.where(iota((nb, toks), 0) % entries == j, list_ref[j], token)
+    token = token * BLOCK + iota((nb, toks), 0) // entries
+    pick = (token == iota((nb, toks), 1)).astype(F32).astype(BF16)
+    for j in range(pieces):
+        stage[:, j, :] = dot(pick, hidden_ref[:, j * LANES : (j + 1) * LANES])
+    out1[...] = stage[...].astype(BF16).reshape(out1.shape)
 
     k_load.wait()
     v_load.wait()
@@ -115,7 +138,6 @@
         kv[x, head, 0] = normalize(ck_ref[:, columns].astype(F32)).astype(BF16)
         kv[x, head, 1] = cv_ref[:, columns]
     w_load.wait()
-    hidden_load.wait()
 
     pl.semaphore_wait(barrier, nb - 1 + nu - 1 + 1)
 
@@ -125,7 +147,56 @@
     each(1, nb, lambda k: list_copy(k, b).start())
     cleanup.append(lambda: each(1, nb, lambda k: list_copy(k, b).wait_send()))
 
-    prev_x, next_x = lax.rem(x + nx - 1, nx), lax.rem(x + 1, nx)
+    def p1_copy(k, slot):
+        to = y_of(k)
+        dev = (x * ny + to, u, c)
+        return remote(out1.at[to], in1.at[slot], p1_s.at[k], p1_r.at[slot], dev)
+
+    each(1, ny, lambda k: p1_copy(k, y).start())
+    cleanup.append(lambda: each(1, ny, lambda k: p1_copy(k, y).wait_send()))
+    in1[y] = out1[y]
+
+    w_out = remote(w_buf.at[c], w_buf.at[c], w_s, w_r, (b, u, other))
+    w_out.start()
+    cleanup.append(w_out.wait_send)
+
+    each(1, nb, lambda k: list_copy(k, bal_of(k)).wait_recv())
+    table = lists[...].reshape(nb, LANES).astype(F32)
+    counts = table[:, :nb]
+    sub_n, lane_n = iota((nb, nb), 0), iota((nb, nb), 1)
+    source = x * ny + lane_n // entries
+    rank = jnp.sum(jnp.where(sub_n < source, counts, 0.0), axis=0, keepdims=True).astype(jnp.int32)
+    known = jnp.sum(jnp.where(sub_n == source, counts, 0.0), axis=0, keepdims=True).astype(jnp.int32)
+    entry = iota((1, nb), 1) % entries
+    slots = nb // nx
+    wanted = (sub_n % slots) * nx + sub_n // slots
+    sel = (rank + entry == wanted) & (entry < known)
+    sel = sel.astype(F32).astype(BF16)
+
+    near = (iota((BLOCK, nb), 1) == iota((BLOCK, nb), 0) * ny + y) & (iota((BLOCK, nb), 0) < nx)
+    named[u] = dot(near.astype(F32).astype(BF16), table.astype(BF16))
+
+    def name_copy(k, slot):
+        return remote(named.at[u], named.at[slot], name_s.at[k], name_r.at[slot], z_dev(k))
+
+    each(1, nu, lambda k: name_copy(k, u).start())
+    cleanup.append(lambda: each(1, nu, lambda k: name_copy(k, u).wait_send()))
+    each(1, ny, lambda k: p1_copy(k, y_of(k)).wait_recv())
+    stage[...] = in1[...].astype(F32).reshape(stage.shape)
+    for j in range(pieces):
+        part = dot(sel, stage[:, j, :].astype(BF16)).astype(BF16)
+        for k in range(nx):
+            outx[k, :, j * LANES : (j + 1) * LANES] = part[k * slots : (k + 1) * slots, :]
+
+    def px_copy(k, slot):
+        to = x_of(k)
+        return remote(outx.at[to], inx.at[slot], px_s.at[k], px_r.at[slot], (to * ny + y, u, c))
+
+    each(1, nx, lambda k: px_copy(k, x).start())
+    cleanup.append(lambda: each(1, nx, lambda k: px_copy(k, x).wait_send()))
+    inx[x] = outx[x]
+
+    prev_x, next_x, far_x = lax.rem(x + nx - 1, nx), lax.rem(x + 1, nx), lax.rem(x + nx // 2, nx)
 
     def ring(slot_x, s, way):
         return remote(kv.at[slot_x], kv.at[slot_x], kv_s.at[s], kv_r.at[slot_x], x_dev(way))
@@ -138,51 +209,12 @@
     own_up.start()
     own_down.start()
     cleanup.extend((own_up.wait_send, own_down.wait_send))
-    w_out = remote(w_buf.at[c], w_buf.at[c], w_s, w_r, (b, u, other))
-    w_out.start()
-    cleanup.append(w_out.wait_send)
-
-    dest = iota((nb, toks), 0)
-    each(1, nb, lambda k: list_copy(k, lax.rem(b + k, nb)).wait_recv())
-    table = lists[...].reshape(nb, LANES).astype(F32)
-    sub_n, lane_n = iota((nb, nb), 0), iota((nb, nb), 1)
-    my_start = jnp.sum(jnp.where(iota((nb, LANES), 0) < b, table, 0.0), axis=0, keepdims=True)
-    my_start = my_start.astype(jnp.int32)
-    local = jnp.bitwise_and(dest - my_start[:, :toks], nb - 1)
-    entry = local // BLOCK
-    token = jnp.zeros((nb, toks), jnp.int32)
-    for j in range(entries):
-        token = jnp.where(entry == j, list_ref[j], token)
-    token = token * BLOCK + local % BLOCK
-    pick = (token == iota((nb, toks), 1)).astype(F32).astype(BF16)
-    for j in range(pieces):
-        stage[:, j, :] = dot(pick, hidden_ref[:, j * LANES : (j + 1) * LANES])
-    out1[...] = stage[...].astype(BF16)
-
-    def p1_copy(k, slot):
-        to = lax.rem(b + k, nb)
-        return remote(out1.at[to], in1.at[slot], p1_s.at[k], p1_r.at[slot], bal_dev(k))
-
-    each(1, nb, lambda k: p1_copy(k, b).start())
-    cleanup.append(lambda: each(1, nb, lambda k: p1_copy(k, b).wait_send()))
-    in1[b] = out1[b]
-
-    counts = table[:, :nb]
-    start_row = jnp.sum(jnp.where(sub_n < lane_n, counts, 0.0), axis=0, keepdims=True).astype(jnp.int32)
-    count_row = jnp.sum(jnp.where(sub_n == lane_n, counts, 0.0), axis=0, keepdims=True)
-    start_col = jnp.sum(jnp.where(lane_n < sub_n, count_row, 0.0), axis=1, keepdims=True).astype(jnp.int32)
-    count_row = count_row.astype(jnp.int32)
-    count_col = counts[:, :BLOCK].astype(jnp.int32)
-    local_row = jnp.bitwise_and(b - start_row, nb - 1)
-    slot_row = (start_row + local_row) // nb
-    sel = (local_row < count_row) & (slot_row == iota((BLOCK, nb), 0))
-    sel = sel.astype(F32).astype(BF16)
-    near = (iota((BLOCK, nb), 1) == iota((BLOCK, nb), 0) * ny + y) & (iota((BLOCK, nb), 0) < nx)
-    xbuf[u, :, width:] = dot(near.astype(F32).astype(BF16), table.astype(BF16)).astype(BF16)
-    each(1, nb, lambda k: p1_copy(k, lax.rem(b + k, nb)).wait_recv())
-    stage[...] = in1[...].astype(F32)
-    for j in range(pieces):
-        xbuf[u, :, j * LANES : (j + 1) * LANES] = dot(sel, stage[:, j, :].astype(BF16)).astype(BF16)
+
+    each(1, nx, lambda k: px_copy(k, x_of(k)).wait_recv())
+    gathered = inx[0].astype(F32)
+    for k in range(1, nx):
+        gathered = gathered + inx[k].astype(F32)
+    xbuf[u] = gathered.astype(BF16)
 
     def z_copy(k, slot):
         return remote(xbuf.at[u], xbuf.at[slot], z_s.at[k], z_r.at[slot], z_dev(k))
@@ -194,12 +226,35 @@
         z_copy(k, u).start()
     cleanup.append(lambda: each(1, nu, lambda k: z_copy(k, u).wait_send()))
 
+    span = nx * keys
+    owner_hit = (iota((keys, nu), 0) // toks == iota((keys, nu), 1)).astype(F32).astype(BF16)
+    block_hit = (iota((keys, LANES), 0) % toks) // BLOCK == iota((keys, LANES), 1)
+    ones = jnp.ones((LANES, LANES), BF16)
+    lane_u = iota((nu, LANES), 1).astype(F32)
+
+    def weigh_values(k):
+        ids = named[:, pl.ds(k, 1), :].reshape(nu, LANES)
+        hit = jnp.zeros((nu, LANES), F32)
+        for j in range(LANES - entries, LANES):
+            hit = hit + (ids[:, j : j + 1] == lane_u).astype(F32)
+        spread = jnp.where(block_hit, dot(owner_hit, hit.astype(BF16)), 0.0).astype(BF16)
+        mask = 1.0 - dot(spread, ones)
+        rows = pl.ds(pl.multiple_of(k * keys, keys), keys)
+        for h in range(2):
+            vaug[h, rows, :HEAD_DIM] = (kv[k, h, 1].astype(F32) * mask).astype(BF16)
+            vaug[h, rows, HEAD_DIM:] = mask.astype(BF16)
+
+    each(1, nu, lambda k: name_copy(k, lax.rem(u + k, nu)).wait_recv())
+    weigh_values(x)
+
     ring(prev_x, 0, 1).wait_recv()
     ring(next_x, 0, 1).wait_recv()
     on_up, on_down = ring_head(prev_x, 0, 2, 1), ring_head(next_x, 1, 3, nx - 1)
     on_up.start()
     on_down.start()
     cleanup.extend((on_up.wait_send, on_down.wait_send))
+    weigh_values(prev_x)
+    weigh_values(next_x)
     w_out.wait_recv()
     gain_load.wait()
 
@@ -232,26 +287,9 @@
     cleanup.append(lambda: each(1, ny, lambda k: q_copy(k, y).wait_send()))
     cleanup.append(lambda: each(1, nx, lambda k: kf_copy(k, x).wait_send()))
 
-    far_x = lax.rem(x + nx // 2, nx)
     ring_head(far_x, 0, 2, 1).wait_recv()
     ring_head(far_x, 1, 3, nx - 1).wait_recv()
-    span = nx * keys
-    owner_hit = (iota((keys, nu), 0) // toks == iota((keys, nu), 1)).astype(F32).astype(BF16)
-    block_hit = (iota((keys, LANES), 0) % toks) // BLOCK == iota((keys, LANES), 1)
-    ones = jnp.ones((LANES, LANES), BF16)
-    lane_u = iota((nu, LANES), 1).astype(F32)
-    extra = xbuf[:, :, width:].astype(F32)
-    for k in range(nx):
-        named = extra[:, k, :]
-        hit = jnp.zeros((nu, LANES), F32)
-        for j in range(LANES - entries, LANES):
-            hit = hit + (named[:, j : j + 1] == lane_u).astype(F32)
-        spread = jnp.where(block_hit, dot(owner_hit, hit.astype(BF16)), 0.0).astype(BF16)
-        mask = 1.0 - dot(spread, ones)
-        rows = pl.ds(k * keys, keys)
-        for h in range(2):
-            vaug[h, rows, :HEAD_DIM] = (kv[k, h, 1].astype(F32) * mask).astype(BF16)
-            vaug[h, rows, HEAD_DIM:] = mask.astype(BF16)
+    weigh_values(far_x)
 
     each(1, nx, lambda k: kf_copy(k, lax.rem(x + k, nx)).wait_recv())
     fresh_keys = nx * half
@@ -325,8 +363,11 @@
     each(1, nu, lambda k: ret_copy(k, u).start())
     cleanup.append(lambda: each(1, nu, lambda k: ret_copy(k, u).wait_send()))
     ret1[u] = ret_out[u]
-    slot_col = start_col + jnp.bitwise_and(b - start_col, nb - 1)
-    give = (slot_col < start_col + count_col) & (slot_col // nb == iota((nb, BLOCK), 1))
+    count_row = jnp.sum(jnp.where(sub_n == lane_n, counts, 0.0), axis=0, keepdims=True)
+    start_col = jnp.sum(jnp.where(lane_n < sub_n, count_row, 0.0), axis=1, keepdims=True).astype(jnp.int32)
+    rank_col = start_col + jnp.bitwise_and(x - start_col, nx - 1)
+    give = rank_col < start_col + counts[:, :slots].astype(jnp.int32)
+    give = give & (rank_col // nx == iota((nb, slots), 1))
     give = give.astype(F32).astype(BF16)
     each(1, nu, lambda k: ret_copy(k, lax.rem(u + k, nu)).wait_recv())
     for h in range(nh):
@@ -334,16 +375,17 @@
     out2[...] = stage2[...].astype(BF16)
 
     def back_copy(k, slot):
-        to = lax.rem(b + k, nb)
-        return remote(out2.at[to], in2.at[slot], back_s.at[k], back_r.at[slot], bal_dev(k))
+        to = bal_of(k)
+        return remote(out2.at[to], in2.at[slot], back_s.at[k], back_r.at[slot], (to, u, c))
 
     each(1, nb, lambda k: back_copy(k, b).start())
     cleanup.append(lambda: each(1, nb, lambda k: back_copy(k, b).wait_send()))
     in2[b] = out2[b]
-    spread_rows = iota((nb, nb), 0)
-    final = jnp.bitwise_and(my_start[:, :nb] + spread_rows, nb - 1) == lane_n
-    final = (final & (spread_rows < my_rows)).astype(F32).astype(BF16)
-    each(1, nb, lambda k: back_copy(k, lax.rem(b + k, nb)).wait_recv())
+    my_start = jnp.sum(jnp.where(sub_n < b, counts, 0.0), axis=0, keepdims=True).astype(jnp.int32)
+    from_x = jnp.bitwise_and(my_start + sub_n // BLOCK, nx - 1)
+    final = (from_x * ny + sub_n % BLOCK == lane_n) & (sub_n // BLOCK < my_blocks)
+    final = final.astype(F32).astype(BF16)
+    each(1, nb, lambda k: back_copy(k, bal_of(k)).wait_recv())
     stage2[...] = in2[...].astype(F32)
     for h in range(nh):
         out_ref[:, h * HEAD_DIM : (h + 1) * HEAD_DIM] = dot(final, stage2[:, h, :].astype(BF16)).astype(BF16)
@@ -380,10 +422,13 @@
             pltpu.VMEM((keys, 2 * HEAD_DIM), BF16),
             pltpu.VMEM((keys, 2 * HEAD_DIM), BF16),
             pltpu.VMEM((nb, 1, LANES), jnp.int32),
+            pltpu.VMEM((nu, BLOCK, LANES), F32),
             pltpu.VMEM((nb, pieces, LANES), F32),
-            pltpu.VMEM((nb, pieces, LANES), BF16),
-            pltpu.VMEM((nb, pieces, LANES), BF16),
-            pltpu.VMEM((nu, BLOCK, width + LANES), BF16),
+            pltpu.VMEM((ny, entries, pieces, LANES), BF16),
+            pltpu.VMEM((ny, entries, pieces, LANES), BF16),
+            pltpu.VMEM((nx, nb // nx, width), BF16),
+            pltpu.VMEM((nx, nb // nx, width), BF16),
+            pltpu.VMEM((nu, nb // nx, width), BF16),
             pltpu.VMEM((nx, 2, 2, keys, HEAD_DIM), BF16),
             pltpu.VMEM((ny, 2 * half, HEAD_DIM), BF16),
             pltpu.VMEM((nx, 2, 2 * half, HEAD_DIM), BF16),
@@ -398,7 +443,9 @@
             dma((6,)),
             dma, dma,
             dma((nb,)), dma((nb,)),
-            dma((nb,)), dma((nb,)),
+            dma((nu,)), dma((nu,)),
+            dma((ny,)), dma((ny,)),
+            dma((nx,)), dma((nx,)),
             dma((nu,)), dma((nu,)),
             dma((4,)), dma((nx + 2,)),
             dma((ny,)), dma((ny,)),

time: 75.6 us -> 77 us (1.019)
  Pallas kernels: 73.9 us -> 75.3 us
    pallas_call x1, Pallas kernels: 73.9 us -> 75.3 us  [on_device(): pl.pallas_call(functools.partial(kernel, nx, nu), out_shape=jax.ShapeDtyp...]
where the time goes in v3:
time: 77 us; the launch traced here: 76.8 us
  Pallas kernels  75.3 us (98%)
  local copies, waits for them, and re-layouts  1.57 us (2%)
    pallas_call x1, Pallas kernels, on_device(): pl.pallas_call(functools.partial(kernel, nx, nu), out_shape=jax.ShapeDtyp...  75.3 us
    unnamed x1, local copies, waits for them, and re-layouts  1.57 us

profile of v3, /device:TPU:8, one launch (start us, length us, event | category | flops | bytes accessed | tf_op | source)
XLA Modules:
  0.0 76.8 jit_solution(7058163423184216651)
XLA Ops:
  0.0 75.3 %shard_map.64 = bf16[32,2048]{1,0:T(8,128)(2,1)} custom-call(s32[4]{0:T(128)} %bitcast.11, bf16[64,3072]{1,0:T(8,128)(2,1)} %bitcast.7, bf16[3072,384]{1,0:T(8,128)(2,1)} %w_in.1, f32[2,128]{1,0:T(2,128)} %bitcast.10, bf16[512,256]{1,0:T(8,128)(2,1)} %bitcast.8, bf16[512,256]{1,0:T(8,128)(2,1)} %bitcast.9), custom_call_target="tpu_custom_call" | custom-call | tf_op jit(solution)/shard_map/pallas_call | solution.py:410
  75.3 1.6 %copy.8 = bf16[1,1,1,32,2048]{4,3,2,1,0:T(8,128)(2,1)} copy(bf16[1,1,1,32,2048]{4,3,2,1,0:T(8,128)(2,1)} %bitcast.6) | data formatting | bytes 262144

commit v4 on v3

--- a/solution.py
+++ b/solution.py
@@ -160,6 +160,20 @@
     w_out.start()
     cleanup.append(w_out.wait_send)
 
+    prev_x, next_x, far_x = lax.rem(x + nx - 1, nx), lax.rem(x + 1, nx), lax.rem(x + nx // 2, nx)
+
+    def ring(slot_x, head, s, way):
+        part = kv.at[slot_x, head]
+        return remote(part, part, kv_s.at[s], kv_r.at[slot_x, head], x_dev(way))
+
+    def ring_start(head):
+        up, down = ring(x, head, 2 * head, 1), ring(x, head, 2 * head + 1, nx - 1)
+        up.start()
+        down.start()
+        cleanup.extend((up.wait_send, down.wait_send))
+
+    ring_start(0)
+
     each(1, nb, lambda k: list_copy(k, bal_of(k)).wait_recv())
     table = lists[...].reshape(nb, LANES).astype(F32)
     counts = table[:, :nb]
@@ -196,19 +210,7 @@
     cleanup.append(lambda: each(1, nx, lambda k: px_copy(k, x).wait_send()))
     inx[x] = outx[x]
 
-    prev_x, next_x, far_x = lax.rem(x + nx - 1, nx), lax.rem(x + 1, nx), lax.rem(x + nx // 2, nx)
-
-    def ring(slot_x, s, way):
-        return remote(kv.at[slot_x], kv.at[slot_x], kv_s.at[s], kv_r.at[slot_x], x_dev(way))
-
-    def ring_head(slot_x, head, s, way):
-        part = kv.at[slot_x, head]
-        return remote(part, part, kv_s.at[s], kv_r.at[nx + head], x_dev(way))
-
-    own_up, own_down = ring(x, 0, 1), ring(x, 1, nx - 1)
-    own_up.start()
-    own_down.start()
-    cleanup.extend((own_up.wait_send, own_down.wait_send))
+    ring_start(1)
 
     each(1, nx, lambda k: px_copy(k, x_of(k)).wait_recv())
     gathered = inx[0].astype(F32)
@@ -247,12 +249,14 @@
     each(1, nu, lambda k: name_copy(k, lax.rem(u + k, nu)).wait_recv())
     weigh_values(x)
 
-    ring(prev_x, 0, 1).wait_recv()
-    ring(next_x, 0, 1).wait_recv()
-    on_up, on_down = ring_head(prev_x, 0, 2, 1), ring_head(next_x, 1, 3, nx - 1)
+    on_up, on_down = ring(prev_x, 0, 4, 1), ring(next_x, 1, 5, nx - 1)
+    ring(prev_x, 0, 0, 1).wait_recv()
     on_up.start()
+    ring(next_x, 1, 2, 1).wait_recv()
     on_down.start()
     cleanup.extend((on_up.wait_send, on_down.wait_send))
+    ring(prev_x, 1, 2, 1).wait_recv()
+    ring(next_x, 0, 0, 1).wait_recv()
     weigh_values(prev_x)
     weigh_values(next_x)
     w_out.wait_recv()
@@ -287,8 +291,8 @@
     cleanup.append(lambda: each(1, ny, lambda k: q_copy(k, y).wait_send()))
     cleanup.append(lambda: each(1, nx, lambda k: kf_copy(k, x).wait_send()))
 
-    ring_head(far_x, 0, 2, 1).wait_recv()
-    ring_head(far_x, 1, 3, nx - 1).wait_recv()
+    ring(far_x, 0, 4, 1).wait_recv()
+    ring(far_x, 1, 5, nx - 1).wait_recv()
     weigh_values(far_x)
 
     each(1, nx, lambda k: kf_copy(k, lax.rem(x + k, nx)).wait_recv())
@@ -447,7 +451,7 @@
             dma((ny,)), dma((ny,)),
             dma((nx,)), dma((nx,)),
             dma((nu,)), dma((nu,)),
-            dma((4,)), dma((nx + 2,)),
+            dma((6,)), dma((nx, 2)),
             dma((ny,)), dma((ny,)),
             dma((nx,)), dma((nx,)),
             dma((ny,)), dma((ny,)),

time: 77 us -> 72 us (0.935)
  Pallas kernels: 75.3 us -> 70.2 us
    pallas_call x1, Pallas kernels: 75.3 us -> 70.2 us  [on_device(): pl.pallas_call(functools.partial(kernel, nx, nu), out_shape=jax.ShapeDtyp...]
where the time goes in v4:
time: 72 us; the launch traced here: 71.8 us
  Pallas kernels  70.2 us (98%)
  local copies, waits for them, and re-layouts  1.57 us (2%)
    pallas_call x1, Pallas kernels, on_device(): pl.pallas_call(functools.partial(kernel, nx, nu), out_shape=jax.ShapeDtyp...  70.2 us
    unnamed x1, local copies, waits for them, and re-layouts  1.57 us

profile of v4, /device:TPU:8, one launch (start us, length us, event | category | flops | bytes accessed | tf_op | source)
XLA Modules:
  0.0 71.8 jit_solution(11019083323143382261)
XLA Ops:
  0.0 70.2 %shard_map.64 = bf16[32,2048]{1,0:T(8,128)(2,1)} custom-call(s32[4]{0:T(128)} %bitcast.11, bf16[64,3072]{1,0:T(8,128)(2,1)} %bitcast.7, bf16[3072,384]{1,0:T(8,128)(2,1)} %w_in.1, f32[2,128]{1,0:T(2,128)} %bitcast.10, bf16[512,256]{1,0:T(8,128)(2,1)} %bitcast.8, bf16[512,256]{1,0:T(8,128)(2,1)} %bitcast.9), custom_call_target="tpu_custom_call" | custom-call | tf_op jit(solution)/shard_map/pallas_call | solution.py:414
  70.2 1.6 %copy.8 = bf16[1,1,1,32,2048]{4,3,2,1,0:T(8,128)(2,1)} copy(bf16[1,1,1,32,2048]{4,3,2,1,0:T(8,128)(2,1)} %bitcast.6) | data formatting | bytes 262144

commit v5 on v4

--- a/solution.py
+++ b/solution.py
@@ -37,7 +37,7 @@
     nx, nu, list_in, hidden_in, w_in, gain_in, ck_in, cv_in, out_ref,
     list_ref, hidden_ref, w_buf, gain_ref, ck_ref, cv_ref, lists, named, stage, out1, in1, outx, inx, xbuf, kv, qbuf, kvf,
     vaug, rsout, rsin, ret_out, ret1, stage2, out2, in2,
-    in_sem, w_s, w_r, list_s, list_r, name_s, name_r, p1_s, p1_r, px_s, px_r, z_s, z_r, kv_s, kv_r, q_s, q_r, kf_s, kf_r, rs_s, rs_r,
+    in_sem, w_s, w_r, list_s, list_r, name_s, name_r, p1_s, p1_r, px_s, px_r, z_s, z_r, opp_s, opp_r, kv_s, kv_r, q_s, q_r, kf_s, kf_r, rs_s, rs_r,
     ret_s, ret_r, back_s, back_r,
 ):
     b, u, c = lax.axis_index("bal"), lax.axis_index("uly"), lax.axis_index("cfg")
@@ -221,12 +221,15 @@
     def z_copy(k, slot):
         return remote(xbuf.at[u], xbuf.at[slot], z_s.at[k], z_r.at[slot], z_dev(k))
 
-    order = []
-    for k in range(nu // 2, 0, -1):
-        order += [k] if 2 * k == nu else [k, nu - k]
+    far = nu // 2
+    order = [far - 1, far + 1, 2, nu - 2, 1, nu - 1]
     for k in order:
         z_copy(k, u).start()
-    cleanup.append(lambda: each(1, nu, lambda k: z_copy(k, u).wait_send()))
+        cleanup.append(z_copy(k, u).wait_send)
+
+    def opposite_copy(side, slot):
+        part = xbuf.at[slot, :, pl.ds(side * (width // 2), width // 2)]
+        return remote(part, part, opp_s.at[side], opp_r.at[side], z_dev(1 if side == 0 else nu - 1))
 
     span = nx * keys
     owner_hit = (iota((keys, nu), 0) // toks == iota((keys, nu), 1)).astype(F32).astype(BF16)
@@ -250,11 +253,16 @@
     weigh_values(x)
 
     on_up, on_down = ring(prev_x, 0, 4, 1), ring(next_x, 1, 5, nx - 1)
+    cleanup.extend((on_up.wait_send, on_down.wait_send))
     ring(prev_x, 0, 0, 1).wait_recv()
     on_up.start()
+    for side, k in enumerate((far + 1, far - 1)):
+        slot = lax.rem(u + k, nu)
+        z_copy(k, slot).wait_recv()
+        opposite_copy(side, slot).start()
+        cleanup.append(opposite_copy(side, slot).wait_send)
     ring(next_x, 1, 2, 1).wait_recv()
     on_down.start()
-    cleanup.extend((on_up.wait_send, on_down.wait_send))
     ring(prev_x, 1, 2, 1).wait_recv()
     ring(next_x, 0, 0, 1).wait_recv()
     weigh_values(prev_x)
@@ -262,7 +270,10 @@
     w_out.wait_recv()
     gain_load.wait()
 
-    each(1, nu, lambda k: z_copy(k, lax.rem(u + k, nu)).wait_recv())
+    for k in order[2:]:
+        z_copy(k, lax.rem(u + k, nu)).wait_recv()
+    for side in range(2):
+        opposite_copy(side, lax.rem(u + far, nu)).wait_recv()
     chunk = math.gcd(width, 1024)
     projected = [jnp.zeros((half, 3 * HEAD_DIM), F32)] * 2
     for j in range(0, width, chunk):
@@ -279,7 +290,7 @@
     def kf_copy(k, slot):
         return remote(kvf.at[x], kvf.at[slot], kf_s.at[k], kf_r.at[slot], x_dev(k))
 
-    for k in range(1, ny // 2 + 1):
+    for k in range(ny // 2, 0, -1):
         for way in [k] if 2 * k == ny else [k, ny - k]:
             q_copy(way, y).start()
     for h in range(2):
@@ -311,14 +322,17 @@
         return remote(rsout.at[to], rsin.at[slot], rs_s.at[k], rs_r.at[slot], y_dev(k))
 
     def attend(i):
-        way_a, way_b = lax.rem(ny - i, ny), i + 1
+        step = ny // 2 - 1 - i
+        last = step == ny // 2 - 1
+        way_a, way_b = step + 1, jnp.where(last, 0, ny - 1 - step)
         slot_a, slot_b = lax.rem(y + way_a, ny), lax.rem(y + way_b, ny)
 
-        @pl.when(i > 0)
+        q_copy(way_a, slot_a).wait_recv()
+
+        @pl.when(jnp.logical_not(last))
         def _():
-            q_copy(way_a, slot_a).wait_recv()
-
-        q_copy(way_b, slot_b).wait_recv()
+            q_copy(way_b, slot_b).wait_recv()
+
         flat_a = jnp.zeros((1, LANES), F32)
         flat_b = jnp.zeros((1, LANES), F32)
         for h in range(2):
@@ -340,18 +354,21 @@
             rest = jnp.where(tail_row == 1, flat - coarse, 0.0)
             rsout[slot, 2 * half :, :] = jnp.where(tail_row == 0, coarse, rest).astype(BF16)
 
-        @pl.when(i > 0)
+        rs_copy(way_a, y).start()
+
+        @pl.when(jnp.logical_not(last))
         def _():
-            rs_copy(way_a, y).start()
-
-        rs_copy(way_b, y).start()
+            rs_copy(way_b, y).start()
 
     each(0, ny // 2, attend)
     cleanup.append(lambda: each(1, ny, lambda k: rs_copy(k, y).wait_send()))
-    rsin[y] = rsout[y]
-
-    each(1, ny, lambda k: rs_copy(k, lax.rem(y + k, ny)).wait_recv())
-    summed = jnp.sum(rsin[...].astype(F32), axis=0)
+
+    summed = rsout[y].astype(F32)
+    for k in range(1, ny // 2 + 1):
+        for way in [k] if 2 * k == ny else [k, ny - k]:
+            slot = lax.rem(y + way, ny)
+            rs_copy(way, slot).wait_recv()
+            summed = summed + rsin[slot].astype(F32)
     total = summed[2 * half : 2 * half + 1, :] + summed[2 * half + 1 : 2 * half + 2, :]
     square = iota((2 * half, LANES), 0) == iota((2 * half, LANES), 1)
     total = jnp.sum(jnp.where(square, total, 0.0), axis=1, keepdims=True)
@@ -451,6 +468,7 @@
             dma((ny,)), dma((ny,)),
             dma((nx,)), dma((nx,)),
             dma((nu,)), dma((nu,)),
+            dma((2,)), dma((2,)),
             dma((6,)), dma((nx, 2)),
             dma((ny,)), dma((ny,)),
             dma((nx,)), dma((nx,)),

time: 72 us -> 68.8 us (0.956)
  Pallas kernels: 70.2 us -> 67.1 us
    pallas_call x1, Pallas kernels: 70.2 us -> 67.1 us  [on_device(): pl.pallas_call(functools.partial(kernel, nx, nu), out_shape=jax.ShapeDtyp...]
where the time goes in v5:
time: 68.8 us; the launch traced here: 68.7 us
  Pallas kernels  67.1 us (98%)
  local copies, waits for them, and re-layouts  1.57 us (2%)
    pallas_call x1, Pallas kernels, on_device(): pl.pallas_call(functools.partial(kernel, nx, nu), out_shape=jax.ShapeDtyp...  67.1 us
    unnamed x1, local copies, waits for them, and re-layouts  1.57 us

profile of v5, /device:TPU:8, one launch (start us, length us, event | category | flops | bytes accessed | tf_op | source)
XLA Modules:
  0.0 68.7 jit_solution(14318563624005420478)
XLA Ops:
  0.0 67.1 %shard_map.64 = bf16[32,2048]{1,0:T(8,128)(2,1)} custom-call(s32[4]{0:T(128)} %bitcast.11, bf16[64,3072]{1,0:T(8,128)(2,1)} %bitcast.7, bf16[3072,384]{1,0:T(8,128)(2,1)} %w_in.1, f32[2,128]{1,0:T(2,128)} %bitcast.10, bf16[512,256]{1,0:T(8,128)(2,1)} %bitcast.8, bf16[512,256]{1,0:T(8,128)(2,1)} %bitcast.9), custom_call_target="tpu_custom_call" | custom-call | tf_op jit(solution)/shard_map/pallas_call | solution.py:431
  67.1 1.6 %copy.8 = bf16[1,1,1,32,2048]{4,3,2,1,0:T(8,128)(2,1)} copy(bf16[1,1,1,32,2048]{4,3,2,1,0:T(8,128)(2,1)} %bitcast.6) | data formatting | bytes 262144

commit v6 on v5

--- a/solution.py
+++ b/solution.py
@@ -78,6 +78,9 @@
     def z_dev(k):
         return (b, lax.rem(u + k, nu), c)
 
+    def z_of(k):
+        return lax.rem(u + farthest(k - 1, nu), nu)
+
     def remote(src, dst, s, r, dev):
         return pltpu.make_async_remote_copy(
             src_ref=src, dst_ref=dst, send_sem=s, recv_sem=r, device_id=dev, device_id_type=MESH
@@ -187,14 +190,6 @@
     sel = (rank + entry == wanted) & (entry < known)
     sel = sel.astype(F32).astype(BF16)
 
-    near = (iota((BLOCK, nb), 1) == iota((BLOCK, nb), 0) * ny + y) & (iota((BLOCK, nb), 0) < nx)
-    named[u] = dot(near.astype(F32).astype(BF16), table.astype(BF16))
-
-    def name_copy(k, slot):
-        return remote(named.at[u], named.at[slot], name_s.at[k], name_r.at[slot], z_dev(k))
-
-    each(1, nu, lambda k: name_copy(k, u).start())
-    cleanup.append(lambda: each(1, nu, lambda k: name_copy(k, u).wait_send()))
     each(1, ny, lambda k: p1_copy(k, y_of(k)).wait_recv())
     stage[...] = in1[...].astype(F32).reshape(stage.shape)
     for j in range(pieces):
@@ -210,6 +205,14 @@
     cleanup.append(lambda: each(1, nx, lambda k: px_copy(k, x).wait_send()))
     inx[x] = outx[x]
 
+    near = (iota((BLOCK, nb), 1) == iota((BLOCK, nb), 0) * ny + y) & (iota((BLOCK, nb), 0) < nx)
+    named[u] = dot(near.astype(F32).astype(BF16), table.astype(BF16))
+
+    def name_copy(k, slot):
+        return remote(named.at[u], named.at[slot], name_s.at[k], name_r.at[slot], z_dev(k))
+
+    each(1, nu, lambda k: name_copy(k, u).start())
+    cleanup.append(lambda: each(1, nu, lambda k: name_copy(k, u).wait_send()))
     ring_start(1)
 
     each(1, nx, lambda k: px_copy(k, x_of(k)).wait_recv())
@@ -275,29 +278,35 @@
     for side in range(2):
         opposite_copy(side, lax.rem(u + far, nu)).wait_recv()
     chunk = math.gcd(width, 1024)
-    projected = [jnp.zeros((half, 3 * HEAD_DIM), F32)] * 2
-    for j in range(0, width, chunk):
-        rows = xbuf[:, :, j : j + chunk].astype(F32).reshape(half, chunk).astype(BF16)
-        projected = [projected[h] + dot(rows, w_buf[h, j : j + chunk, :]) for h in range(2)]
+    starts = range(0, width, chunk)
+    rows = [xbuf[:, :, j : j + chunk].astype(F32).reshape(half, chunk).astype(BF16) for j in starts]
+
+    def project(h, columns):
+        total = dot(rows[0], w_buf[h, :chunk, columns])
+        for i, j in enumerate(starts):
+            if i > 0:
+                total = total + dot(rows[i], w_buf[h, j : j + chunk, columns])
+        return total
+
     for h in range(2):
-        mine = slice(h * half, (h + 1) * half)
-        query = normalize(projected[h][:, :HEAD_DIM]) * gain_ref[h : h + 1, :]
-        qbuf[y, mine, :] = query.astype(BF16)
+        query = normalize(project(h, slice(0, HEAD_DIM))) * gain_ref[h : h + 1, :]
+        qbuf[y, h * half : (h + 1) * half, :] = query.astype(BF16)
 
     def q_copy(k, slot):
         return remote(qbuf.at[y], qbuf.at[slot], q_s.at[k], q_r.at[slot], y_dev(k))
 
     def kf_copy(k, slot):
-        return remote(kvf.at[x], kvf.at[slot], kf_s.at[k], kf_r.at[slot], x_dev(k))
+        return remote(kvf.at[x], kvf.at[slot], kf_s.at[k], kf_r.at[slot], (x_of(k) * ny + y, u, c))
 
     for k in range(ny // 2, 0, -1):
         for way in [k] if 2 * k == ny else [k, ny - k]:
             q_copy(way, y).start()
     for h in range(2):
         mine = slice(h * half, (h + 1) * half)
-        k_fresh = projected[h][:, HEAD_DIM : 2 * HEAD_DIM].astype(BF16).astype(F32)
+        both = project(h, slice(HEAD_DIM, 3 * HEAD_DIM))
+        k_fresh = both[:, :HEAD_DIM].astype(BF16).astype(F32)
         kvf[x, 0, mine, :] = normalize(k_fresh).astype(BF16)
-        kvf[x, 1, mine, :] = projected[h][:, 2 * HEAD_DIM :].astype(BF16)
+        kvf[x, 1, mine, :] = both[:, HEAD_DIM:].astype(BF16)
     each(1, nx, lambda k: kf_copy(k, x).start())
     cleanup.append(lambda: each(1, ny, lambda k: q_copy(k, y).wait_send()))
     cleanup.append(lambda: each(1, nx, lambda k: kf_copy(k, x).wait_send()))
@@ -306,7 +315,7 @@
     ring(far_x, 1, 5, nx - 1).wait_recv()
     weigh_values(far_x)
 
-    each(1, nx, lambda k: kf_copy(k, lax.rem(x + k, nx)).wait_recv())
+    each(1, nx, lambda k: kf_copy(k, x_of(k)).wait_recv())
     fresh_keys = nx * half
     for h in range(2):
         mine = slice(h * half, (h + 1) * half)
@@ -378,8 +387,8 @@
         ret_out[:, h] = rows.reshape(nu, BLOCK, HEAD_DIM).astype(BF16)
 
     def ret_copy(k, slot):
-        to = lax.rem(u + k, nu)
-        return remote(ret_out.at[to], ret1.at[slot], ret_s.at[k], ret_r.at[slot], z_dev(k))
+        to = z_of(k)
+        return remote(ret_out.at[to], ret1.at[slot], ret_s.at[k], ret_r.at[slot], (b, to, c))
 
     each(1, nu, lambda k: ret_copy(k, u).start())
     cleanup.append(lambda: each(1, nu, lambda k: ret_copy(k, u).wait_send()))
@@ -390,7 +399,7 @@
     give = rank_col < start_col + counts[:, :slots].astype(jnp.int32)
     give = give & (rank_col // nx == iota((nb, slots), 1))
     give = give.astype(F32).astype(BF16)
-    each(1, nu, lambda k: ret_copy(k, lax.rem(u + k, nu)).wait_recv())
+    each(1, nu, lambda k: ret_copy(k, z_of(k)).wait_recv())
     for h in range(nh):
         stage2[:, h, :] = dot(give, ret1[h // 2, h % 2])
     out2[...] = stage2[...].astype(BF16)
@@ -454,8 +463,8 @@
             pltpu.VMEM((ny, 2 * half, HEAD_DIM), BF16),
             pltpu.VMEM((nx, 2, 2 * half, HEAD_DIM), BF16),
             pltpu.VMEM((2, span, 2 * HEAD_DIM), BF16),
-            pltpu.VMEM((ny, 2 * half + 16, HEAD_DIM), BF16),
-            pltpu.VMEM((ny, 2 * half + 16, HEAD_DIM), BF16),
+            pltpu.VMEM((ny, 2 * half + 8, HEAD_DIM), BF16),
+            pltpu.VMEM((ny, 2 * half + 8, HEAD_DIM), BF16),
             pltpu.VMEM((nu, 2, BLOCK, HEAD_DIM), BF16),
             pltpu.VMEM((nu, 2, BLOCK, HEAD_DIM), BF16),
             pltpu.VMEM((nb, nh, HEAD_DIM), F32),

time: 68.8 us -> 68.1 us (0.990)
  Pallas kernels: 67.1 us -> 66.4 us
where the time goes in v6:
time: 68.1 us; the launch traced here: 68 us
  Pallas kernels  66.4 us (98%)
  local copies, waits for them, and re-layouts  1.57 us (2%)
    pallas_call x1, Pallas kernels, on_device(): pl.pallas_call(functools.partial(kernel, nx, nu), out_shape=jax.ShapeDtyp...  66.4 us
    unnamed x1, local copies, waits for them, and re-layouts  1.57 us

profile of v6, /device:TPU:8, one launch (start us, length us, event | category | flops | bytes accessed | tf_op | source)
XLA Modules:
  0.0 68.0 jit_solution(9521459073727945434)
XLA Ops:
  0.0 66.4 %shard_map.64 = bf16[32,2048]{1,0:T(8,128)(2,1)} custom-call(s32[4]{0:T(128)} %bitcast.11, bf16[64,3072]{1,0:T(8,128)(2,1)} %bitcast.7, bf16[3072,384]{1,0:T(8,128)(2,1)} %w_in.1, f32[2,128]{1,0:T(2,128)} %bitcast.10, bf16[512,256]{1,0:T(8,128)(2,1)} %bitcast.8, bf16[512,256]{1,0:T(8,128)(2,1)} %bitcast.9), custom_call_target="tpu_custom_call" | custom-call | tf_op jit(solution)/shard_map/pallas_call | solution.py:440
  66.4 1.6 %copy.8 = bf16[1,1,1,32,2048]{4,3,2,1,0:T(8,128)(2,1)} copy(bf16[1,1,1,32,2048]{4,3,2,1,0:T(8,128)(2,1)} %bitcast.6) | data formatting | bytes 262144

commit v7 on v6

--- a/solution.py
+++ b/solution.py
@@ -69,6 +69,15 @@
     def bal_dev(k):
         return (bal_of(k), u, c)
 
+    def ways(n):
+        return [(n // 2 + (j + 1) // 2 * (1 if j % 2 == 1 else -1)) % n for j in range(n)]
+
+    x_list = [lax.rem(x + way, nx) for way in ways(nx)]
+    y_list = [lax.rem(y + way, ny) for way in ways(ny)]
+    bal_list = [x_list[j % nx] * ny + y_list[j // nx] for j in range(nb)]
+
+    z_list = [lax.rem(u + way, nu) for way in ways(nu)]
+
     def x_dev(k):
         return (lax.rem(x + k, nx) * ny + y, u, c)
 
@@ -77,9 +86,6 @@
 
     def z_dev(k):
         return (b, lax.rem(u + k, nu), c)
-
-    def z_of(k):
-        return lax.rem(u + farthest(k - 1, nu), nu)
 
     def remote(src, dst, s, r, dev):
         return pltpu.make_async_remote_copy(
@@ -144,19 +150,21 @@
 
     pl.semaphore_wait(barrier, nb - 1 + nu - 1 + 1)
 
-    def list_copy(k, slot):
-        return remote(lists.at[b], lists.at[slot], list_s.at[k], list_r.at[slot], bal_dev(k))
-
-    each(1, nb, lambda k: list_copy(k, b).start())
-    cleanup.append(lambda: each(1, nb, lambda k: list_copy(k, b).wait_send()))
+    def list_copy(k, slot, to):
+        return remote(lists.at[b], lists.at[slot], list_s.at[k], list_r.at[slot], (to, u, c))
+
+    for k in range(1, nb):
+        list_copy(k, b, bal_list[k - 1]).start()
+    cleanup.append(lambda: each(1, nb, lambda k: list_copy(k, b, bal_of(k)).wait_send()))
 
     def p1_copy(k, slot):
-        to = y_of(k)
+        to = y_list[k - 1]
         dev = (x * ny + to, u, c)
         return remote(out1.at[to], in1.at[slot], p1_s.at[k], p1_r.at[slot], dev)
 
-    each(1, ny, lambda k: p1_copy(k, y).start())
-    cleanup.append(lambda: each(1, ny, lambda k: p1_copy(k, y).wait_send()))
+    for k in range(1, ny):
+        p1_copy(k, y).start()
+        cleanup.append(p1_copy(k, y).wait_send)
     in1[y] = out1[y]
 
     w_out = remote(w_buf.at[c], w_buf.at[c], w_s, w_r, (b, u, other))
@@ -177,7 +185,12 @@
 
     ring_start(0)
 
-    each(1, nb, lambda k: list_copy(k, bal_of(k)).wait_recv())
+
+    def list_arrival(k):
+        slot = lax.rem(b + k, nb)
+        list_copy(k, slot, slot).wait_recv()
+
+    each(1, nb, list_arrival)
     table = lists[...].reshape(nb, LANES).astype(F32)
     counts = table[:, :nb]
     sub_n, lane_n = iota((nb, nb), 0), iota((nb, nb), 1)
@@ -190,7 +203,8 @@
     sel = (rank + entry == wanted) & (entry < known)
     sel = sel.astype(F32).astype(BF16)
 
-    each(1, ny, lambda k: p1_copy(k, y_of(k)).wait_recv())
+    for k in range(1, ny):
+        p1_copy(k, y_list[k - 1]).wait_recv()
     stage[...] = in1[...].astype(F32).reshape(stage.shape)
     for j in range(pieces):
         part = dot(sel, stage[:, j, :].astype(BF16)).astype(BF16)
@@ -198,11 +212,12 @@
             outx[k, :, j * LANES : (j + 1) * LANES] = part[k * slots : (k + 1) * slots, :]
 
     def px_copy(k, slot):
-        to = x_of(k)
+        to = x_list[k - 1]
         return remote(outx.at[to], inx.at[slot], px_s.at[k], px_r.at[slot], (to * ny + y, u, c))
 
-    each(1, nx, lambda k: px_copy(k, x).start())
-    cleanup.append(lambda: each(1, nx, lambda k: px_copy(k, x).wait_send()))
+    for k in range(1, nx):
+        px_copy(k, x).start()
+        cleanup.append(px_copy(k, x).wait_send)
     inx[x] = outx[x]
 
     near = (iota((BLOCK, nb), 1) == iota((BLOCK, nb), 0) * ny + y) & (iota((BLOCK, nb), 0) < nx)
@@ -215,7 +230,8 @@
     cleanup.append(lambda: each(1, nu, lambda k: name_copy(k, u).wait_send()))
     ring_start(1)
 
-    each(1, nx, lambda k: px_copy(k, x_of(k)).wait_recv())
+    for k in range(1, nx):
+        px_copy(k, x_list[k - 1]).wait_recv()
     gathered = inx[0].astype(F32)
     for k in range(1, nx):
         gathered = gathered + inx[k].astype(F32)
@@ -372,6 +388,16 @@
     each(0, ny // 2, attend)
     cleanup.append(lambda: each(1, ny, lambda k: rs_copy(k, y).wait_send()))
 
+    count_row = jnp.sum(jnp.where(sub_n == lane_n, counts, 0.0), axis=0, keepdims=True)
+    start_col = jnp.sum(jnp.where(lane_n < sub_n, count_row, 0.0), axis=1, keepdims=True).astype(jnp.int32)
+    rank_col = start_col + jnp.bitwise_and(x - start_col, nx - 1)
+    give = rank_col < start_col + counts[:, :slots].astype(jnp.int32)
+    give = give & (rank_col // nx == iota((nb, slots), 1))
+    give = give.astype(F32).astype(BF16)
+    my_start = jnp.sum(jnp.where(sub_n < b, counts, 0.0), axis=0, keepdims=True).astype(jnp.int32)
+    from_x = jnp.bitwise_and(my_start + sub_n // BLOCK, nx - 1)
+    final = (from_x * ny + sub_n % BLOCK == lane_n) & (sub_n // BLOCK < my_blocks)
+    final = final.astype(F32).astype(BF16)
     summed = rsout[y].astype(F32)
     for k in range(1, ny // 2 + 1):
         for way in [k] if 2 * k == ny else [k, ny - k]:
@@ -387,41 +413,38 @@
         ret_out[:, h] = rows.reshape(nu, BLOCK, HEAD_DIM).astype(BF16)
 
     def ret_copy(k, slot):
-        to = z_of(k)
+        to = z_list[k - 1]
         return remote(ret_out.at[to], ret1.at[slot], ret_s.at[k], ret_r.at[slot], (b, to, c))
 
-    each(1, nu, lambda k: ret_copy(k, u).start())
-    cleanup.append(lambda: each(1, nu, lambda k: ret_copy(k, u).wait_send()))
+    for k in range(1, nu):
+        ret_copy(k, u).start()
+        cleanup.append(ret_copy(k, u).wait_send)
     ret1[u] = ret_out[u]
-    count_row = jnp.sum(jnp.where(sub_n == lane_n, counts, 0.0), axis=0, keepdims=True)
-    start_col = jnp.sum(jnp.where(lane_n < sub_n, count_row, 0.0), axis=1, keepdims=True).astype(jnp.int32)
-    rank_col = start_col + jnp.bitwise_and(x - start_col, nx - 1)
-    give = rank_col < start_col + counts[:, :slots].astype(jnp.int32)
-    give = give & (rank_col // nx == iota((nb, slots), 1))
-    give = give.astype(F32).astype(BF16)
-    each(1, nu, lambda k: ret_copy(k, z_of(k)).wait_recv())
+    for k in range(1, nu):
+        ret_copy(k, z_list[k - 1]).wait_recv()
     for h in range(nh):
         stage2[:, h, :] = dot(give, ret1[h // 2, h % 2])
     out2[...] = stage2[...].astype(BF16)
 
-    def back_copy(k, slot):
-        to = bal_of(k)
+    def back_copy(k, slot, to):
         return remote(out2.at[to], in2.at[slot], back_s.at[k], back_r.at[slot], (to, u, c))
 
-    each(1, nb, lambda k: back_copy(k, b).start())
-    cleanup.append(lambda: each(1, nb, lambda k: back_copy(k, b).wait_send()))
+    for k in range(1, nb):
+        back_copy(k, b, bal_list[k - 1]).start()
     in2[b] = out2[b]
-    my_start = jnp.sum(jnp.where(sub_n < b, counts, 0.0), axis=0, keepdims=True).astype(jnp.int32)
-    from_x = jnp.bitwise_and(my_start + sub_n // BLOCK, nx - 1)
-    final = (from_x * ny + sub_n % BLOCK == lane_n) & (sub_n // BLOCK < my_blocks)
-    final = final.astype(F32).astype(BF16)
-    each(1, nb, lambda k: back_copy(k, bal_of(k)).wait_recv())
+    for finish in cleanup:
+        finish()
+
+    def back_arrival(k):
+        slot = lax.rem(b + k, nb)
+        back_copy(k, slot, slot).wait_recv()
+
+    each(1, nb, back_arrival)
     stage2[...] = in2[...].astype(F32)
     for h in range(nh):
         out_ref[:, h * HEAD_DIM : (h + 1) * HEAD_DIM] = dot(final, stage2[:, h, :].astype(BF16)).astype(BF16)
 
-    for finish in cleanup:
-        finish()
+    each(1, nb, lambda k: back_copy(k, b, bal_of(k)).wait_send())
 
 
 def on_device(hidden, w_qkv, q_gain, cache_k, cache_v, fresh_list):

time: 68.1 us -> 66.4 us (0.975)
  Pallas kernels: 66.4 us -> 64.7 us
    pallas_call x1, Pallas kernels: 66.4 us -> 64.7 us  [on_device(): pl.pallas_call(functools.partial(kernel, nx, nu), out_shape=jax.ShapeDtyp...]
where the time goes in v7:
time: 66.4 us; the launch traced here: 66.3 us
  Pallas kernels  64.7 us (97%)
  local copies, waits for them, and re-layouts  1.57 us (2%)
    pallas_call x1, Pallas kernels, on_device(): pl.pallas_call(functools.partial(kernel, nx, nu), out_shape=jax.ShapeDtyp...  64.7 us
    unnamed x1, local copies, waits for them, and re-layouts  1.57 us

profile of v7, /device:TPU:8, one launch (start us, length us, event | category | flops | bytes accessed | tf_op | source)
XLA Modules:
  0.0 66.3 jit_solution(16414190947479780596)
XLA Ops:
  0.0 64.7 %shard_map.64 = bf16[32,2048]{1,0:T(8,128)(2,1)} custom-call(s32[4]{0:T(128)} %bitcast.11, bf16[64,3072]{1,0:T(8,128)(2,1)} %bitcast.7, bf16[3072,384]{1,0:T(8,128)(2,1)} %w_in.1, f32[2,128]{1,0:T(2,128)} %bitcast.10, bf16[512,256]{1,0:T(8,128)(2,1)} %bitcast.8, bf16[512,256]{1,0:T(8,128)(2,1)} %bitcast.9), custom_call_target="tpu_custom_call" | custom-call | tf_op jit(solution)/shard_map/pallas_call | solution.py:463
  64.7 1.6 %copy.8 = bf16[1,1,1,32,2048]{4,3,2,1,0:T(8,128)(2,1)} copy(bf16[1,1,1,32,2048]{4,3,2,1,0:T(8,128)(2,1)} %bitcast.6) | data formatting | bytes 262144

commit v8 on v7

--- a/solution.py
+++ b/solution.py
@@ -66,9 +66,6 @@
     def bal_of(k):
         return x_of(lax.rem(k - 1, nx) + 1) * ny + y_of((k - 1) // nx + 1)
 
-    def bal_dev(k):
-        return (bal_of(k), u, c)
-
     def ways(n):
         return [(n // 2 + (j + 1) // 2 * (1 if j % 2 == 1 else -1)) % n for j in range(n)]
 
@@ -116,8 +113,10 @@
     def greet(dev):
         pl.semaphore_signal(barrier, inc=1, device_id=dev, device_id_type=MESH)
 
-    each(1, nb, lambda k: greet(bal_dev(k)))
-    each(1, nu, lambda k: greet(z_dev(k)))
+    for k in range(1, nb):
+        greet((bal_list[k - 1], u, c))
+    for k in range(1, nu):
+        greet((b, z_list[k - 1], c))
     greet((b, u, other))
 
     list_load.wait()
@@ -146,7 +145,6 @@
         columns = slice(head * HEAD_DIM, (head + 1) * HEAD_DIM)
         kv[x, head, 0] = normalize(ck_ref[:, columns].astype(F32)).astype(BF16)
         kv[x, head, 1] = cv_ref[:, columns]
-    w_load.wait()
 
     pl.semaphore_wait(barrier, nb - 1 + nu - 1 + 1)
 
@@ -166,10 +164,6 @@
         p1_copy(k, y).start()
         cleanup.append(p1_copy(k, y).wait_send)
     in1[y] = out1[y]
-
-    w_out = remote(w_buf.at[c], w_buf.at[c], w_s, w_r, (b, u, other))
-    w_out.start()
-    cleanup.append(w_out.wait_send)
 
     prev_x, next_x, far_x = lax.rem(x + nx - 1, nx), lax.rem(x + 1, nx), lax.rem(x + nx // 2, nx)
 
@@ -184,6 +178,11 @@
         cleanup.extend((up.wait_send, down.wait_send))
 
     ring_start(0)
+
+    w_load.wait()
+    w_out = remote(w_buf.at[c], w_buf.at[c], w_s, w_r, (b, u, other))
+    w_out.start()
+    cleanup.append(w_out.wait_send)
 
 
     def list_arrival(k):

time: 66.4 us -> 66 us (level)
  no operation moved by 1% of the time
where the time goes in v8:
time: 66 us; the launch traced here: 65.9 us
  Pallas kernels  64.3 us (97%)
  local copies, waits for them, and re-layouts  1.57 us (2%)
    pallas_call x1, Pallas kernels, on_device(): pl.pallas_call(functools.partial(kernel, nx, nu), out_shape=jax.ShapeDtyp...  64.3 us
    unnamed x1, local copies, waits for them, and re-layouts  1.57 us

profile of v8, /device:TPU:8, one launch (start us, length us, event | category | flops | bytes accessed | tf_op | source)
XLA Modules:
  0.0 65.9 jit_solution(17041424477973639734)
XLA Ops:
  0.0 64.3 %shard_map.64 = bf16[32,2048]{1,0:T(8,128)(2,1)} custom-call(s32[4]{0:T(128)} %bitcast.11, bf16[64,3072]{1,0:T(8,128)(2,1)} %bitcast.7, bf16[3072,384]{1,0:T(8,128)(2,1)} %w_in.1, f32[2,128]{1,0:T(2,128)} %bitcast.10, bf16[512,256]{1,0:T(8,128)(2,1)} %bitcast.8, bf16[512,256]{1,0:T(8,128)(2,1)} %bitcast.9), custom_call_target="tpu_custom_call" | custom-call | tf_op jit(solution)/shard_map/pallas_call | solution.py:462
  64.3 1.6 %copy.8 = bf16[1,1,1,32,2048]{4,3,2,1,0:T(8,128)(2,1)} copy(bf16[1,1,1,32,2048]{4,3,2,1,0:T(8,128)(2,1)} %bitcast.6) | data formatting | bytes 262144

commit v9 on v8

--- a/solution.py
+++ b/solution.py
@@ -189,6 +189,9 @@
         slot = lax.rem(b + k, nb)
         list_copy(k, slot, slot).wait_recv()
 
+    for k in range(1, ny):
+        p1_copy(k, y_list[k - 1]).wait_recv()
+    stage[...] = in1[...].astype(F32).reshape(stage.shape)
     each(1, nb, list_arrival)
     table = lists[...].reshape(nb, LANES).astype(F32)
     counts = table[:, :nb]
@@ -202,9 +205,6 @@
     sel = (rank + entry == wanted) & (entry < known)
     sel = sel.astype(F32).astype(BF16)
 
-    for k in range(1, ny):
-        p1_copy(k, y_list[k - 1]).wait_recv()
-    stage[...] = in1[...].astype(F32).reshape(stage.shape)
     for j in range(pieces):
         part = dot(sel, stage[:, j, :].astype(BF16)).astype(BF16)
         for k in range(nx):

time: 66 us -> 66.4 us (level)
  no operation moved by 1% of the time
where the time goes in v9:
time: 66.4 us; the launch traced here: 66.3 us
  Pallas kernels  64.7 us (97%)
  local copies, waits for them, and re-layouts  1.57 us (2%)
    pallas_call x1, Pallas kernels, on_device(): pl.pallas_call(functools.partial(kernel, nx, nu), out_shape=jax.ShapeDtyp...  64.7 us
    unnamed x1, local copies, waits for them, and re-layouts  1.57 us

profile of v9, /device:TPU:8, one launch (start us, length us, event | category | flops | bytes accessed | tf_op | source)
XLA Modules:
  0.0 66.3 jit_solution(3937841562235847453)
XLA Ops:
  0.0 64.7 %shard_map.64 = bf16[32,2048]{1,0:T(8,128)(2,1)} custom-call(s32[4]{0:T(128)} %bitcast.11, bf16[64,3072]{1,0:T(8,128)(2,1)} %bitcast.7, bf16[3072,384]{1,0:T(8,128)(2,1)} %w_in.1, f32[2,128]{1,0:T(2,128)} %bitcast.10, bf16[512,256]{1,0:T(8,128)(2,1)} %bitcast.8, bf16[512,256]{1,0:T(8,128)(2,1)} %bitcast.9), custom_call_target="tpu_custom_call" | custom-call | tf_op jit(solution)/shard_map/pallas_call | solution.py:462
  64.7 1.6 %copy.8 = bf16[1,1,1,32,2048]{4,3,2,1,0:T(8,128)(2,1)} copy(bf16[1,1,1,32,2048]{4,3,2,1,0:T(8,128)(2,1)} %bitcast.6) | data formatting | bytes 262144
